TPU v7x, 512 devices: a whole 4x8x8 slice. The times are simulated.
512 devices in a mesh: leaf: 128 (over z, y, core), vec: 4 (over x).
Axes of the slice: x: 4, y: 8, z: 8, core: 2. Of those that a mesh axis runs over, the one named last changes fastest.
Arguments:
- vectors: float32 [64, 524288], P('vec', 'leaf'), may hold values from -6 to 6
- points: float32 [2, 524288], P(None, 'leaf'), may hold values from 0 to 1
- bases: float32 [2048, 256, 64], P('leaf'), may hold values from -0.375 to 0.375
- transfer: float32 [6, 2, 64, 64], replicated, may hold values from -0.5 to 0.5
- coupling: float32 [7, 4, 64, 64], replicated, may hold values from -0.375 to 0.375
- near_lists: int32 [2048, 8], P('leaf'), may hold values from 0 to 2047, as said below
- far_lists: int32 [4, 2048, 4], P(None, 'leaf'), may hold values from 0 to 2047, as said below
- coarse_lists: int32 [3, 128, 4], replicated, may hold values from 0 to 127, as said below
Outputs:
- product: float32 [64, 524288], P('vec', 'leaf')
Inputs may be any that keep to these rules, and one draw needn't show every extreme that they name: `near_lists`: row l lists 8 leaves other than l, each within 16 leaves of l. Row d * 16 + j with j below 16 / 2**k of far_lists[k] belongs to node d * (16 / 2**k) + j of level k and lists other nodes of that level within 16 / 2**k of it; all other rows are 0. Row n of coarse_lists[i] for n below 128 / 2**i lists nodes of level 4 + i, any of them; all other rows are 0.
All inputs are finite; a program needn't handle non-finite values.
Results may differ from a plain program's by a relative error of at most 0.0003.
Values sent between devices are 32-bit elements; how exact they have to be, the bound alone decides.
A program may use at most 64 MiB of HBM per device.

v0:
```python
import jax
import jax.numpy as jnp
from jax import lax
from jax.sharding import PartitionSpec as P

highest = lax.Precision.HIGHEST
kernel_width = 0.2
near_weight = 0.0625


def padded(cells, sides, width):
    for axis, dim in sides:
        count = lax.axis_size(axis)
        ends = count - 1
        head = lax.slice_in_dim(cells, 0, width, axis=dim)
        tail = lax.slice_in_dim(cells, cells.shape[dim] - width, cells.shape[dim], axis=dim)
        cells = jnp.concatenate(
            [
                lax.ppermute(tail, axis, [(i, (i + 1) % count) for i in range(ends)]),
                cells,
                lax.ppermute(head, axis, [((i + 1) % count, i) for i in range(ends)]),
            ],
            axis=dim,
        )
    return cells


def kernel(source, target):
    dx = source[0][:, :, None] - target[0][None, None, :]
    dy = source[1][:, :, None] - target[1][None, None, :]
    return near_weight * jnp.exp(-jnp.sqrt(dx * dx + dy * dy) / kernel_width)


def upward(child, pair):
    grouped = child.reshape(child.shape[0] // 2, 2, child.shape[1], child.shape[2])
    return jnp.einsum("nvr,rs->nvs", grouped[:, 0], pair[0], precision=highest) + jnp.einsum(
        "nvr,rs->nvs", grouped[:, 1], pair[1], precision=highest
    )


def downward(parent, pair):
    left = jnp.einsum("nvs,rs->nvr", parent, pair[0], precision=highest)
    right = jnp.einsum("nvs,rs->nvr", parent, pair[1], precision=highest)
    return jnp.stack([left, right], 1).reshape(
        2 * parent.shape[0], parent.shape[1], parent.shape[2]
    )


def far_terms(source, rows, maps):
    total = jnp.einsum("nvr,rs->nvs", source[rows[:, 0]], maps[0], precision=highest)
    for slot in range(1, rows.shape[1]):
        total = total + jnp.einsum(
            "nvr,rs->nvs", source[rows[:, slot]], maps[slot], precision=highest
        )
    return total


def coarse_pass(cut_up, transfer, coupling, lists, cut):
    ups = [cut_up]
    for level in range(1, lists.shape[0]):
        ups.append(upward(ups[-1], transfer[cut + level - 1]))
    result = None
    for level in range(lists.shape[0] - 1, -1, -1):
        count = ups[level].shape[0]
        here = far_terms(ups[level], lists[level, :count], coupling[cut + level])
        result = here if result is None else here + downward(result, transfer[cut + level])
    return result


def local(vectors, points, bases, transfer, coupling, near_lists, far_lists, coarse_lists):
    leaf_dev = bases.shape[0]
    leaf = bases.shape[1]
    cols = vectors.shape[0]
    npts = vectors.shape[1]
    levels_cut = far_lists.shape[0]
    me = lax.axis_index("leaf")
    stacked = jnp.concatenate([vectors, points], 0)
    wide = padded(stacked, (("leaf", 1),), npts)
    wide = wide.reshape(cols + 2, 3 * leaf_dev, leaf)
    blocks = vectors.reshape(cols, leaf_dev, leaf)
    ups = [jnp.einsum("vlp,lpr->lvr", blocks, bases, precision=highest)]
    for level in range(1, levels_cut + 1):
        ups.append(upward(ups[-1], transfer[level - 1]))
    far_parts = []
    for level in range(levels_cut):
        count = leaf_dev >> level
        source = padded(ups[level], (("leaf", 0),), count)
        rows = far_lists[level, :count] - (me - 1) * count
        far_parts.append(far_terms(source, rows, coupling[level]))
    every_cut = lax.all_gather(ups[levels_cut], "leaf", axis=0, tiled=True)
    coarse_down = coarse_pass(every_cut, transfer, coupling, coarse_lists, levels_cut)
    result = lax.dynamic_slice_in_dim(coarse_down, me, 1, 0)
    for level in range(levels_cut - 1, -1, -1):
        result = far_parts[level] + downward(result, transfer[level])
    far_part = jnp.einsum("lvr,lpr->vlp", result, bases, precision=highest).reshape(cols, npts)
    own_rows = near_lists - (me - 1) * leaf_dev

    def one_leaf(inputs):
        index, row = inputs
        picks = jnp.concatenate([jnp.reshape(index + leaf_dev, (1,)), row])
        taken = wide[:, picks, :]
        weights = kernel(taken[cols:], taken[cols:, 0, :])
        return jnp.einsum("vjs,jst->vt", taken[:cols], weights, precision=highest)

    near = lax.map(one_leaf, (jnp.arange(leaf_dev, dtype=jnp.int32), own_rows))
    return far_part + jnp.transpose(near, (1, 0, 2)).reshape(cols, npts)


def solution(mesh):
    in_specs = (
        P("vec", "leaf"),
        P(None, "leaf"),
        P("leaf", None, None),
        P(),
        P(),
        P("leaf", None),
        P(None, "leaf", None),
        P(),
    )
    out_specs = P("vec", "leaf")
    return jax.shard_map(local, mesh=mesh, in_specs=in_specs, out_specs=out_specs, check_vma=False)
```

profile of v0, /device:TPU:260, one launch (start us, length us, event | category | flops | bytes accessed | tf_op | source)
XLA Modules:
  0.0 267.3 jit_solution(10006772442754654871)
XLA Ops:
  0.0 1.2 copy-done
  1.2 1.9 fusion.55
  4.2 0.9 fusion.64
  5.1 1.5 convolution_add_fusion.13
  8.3 1.9 collective-permute-start.6
  10.3 7.0 %collective-permute-start.7 = (f32[2,16,64]{2,1,0:T(8,128)S(1)}, f32[2,16,64]{2,1,0:T(8,128)}, u32[]{:S(2)}, u32[]{:S(2)}) collective-permute-start(f32[2,16,64]{2,1,0:T(8,128)S(1)} %convolution_add_fusion.15), channel_id=1, source_target_pairs={{4,0},{8,4},{12,8},{16,12},{20,16},{24,20},{28,24},{32,28},{36,32}... | collective-permute-start | bytes 24584 | tf_op jit(solution)/shard_map/ppermute | solution.py:21
  17.2 1.9 collective-permute-start.4
  19.2 7.0 %collective-permute-start.5 = (f32[4,16,64]{2,1,0:T(8,128)}, f32[4,16,64]{2,1,0:T(8,128)}, u32[]{:S(2)}, u32[]{:S(2)}) collective-permute-start(f32[4,16,64]{2,1,0:T(8,128)} %convolution_add_fusion.13), channel_id=1, source_target_pairs={{4,0},{8,4},{12,8},{16,12},{20,16},{24,20},{28,24},{32,28},{36,32}... | collective-permute-start | bytes 49160 | tf_op jit(solution)/shard_map/ppermute | solution.py:21
  26.1 1.9 collective-permute-start.2
  29.0 50.0 %all-gather = f32[2048,64]{1,0:T(8,128)S(1)} all-gather(f32[16,64]{1,0:T(8,128)S(1)} %convolution_add_fusion.16), channel_id=2, replica_groups=mesh['leaf'=128,'vec'=4] {'leaf'}, dimensions={0}, use_global_device_ids=true | all-gather | bytes 528384 | tf_op jit(solution)/shard_map/all_gather | solution.py:90
  83.3 1.3 gather_fusion.25
  85.3 1.3 pad_clamp_fusion.1
  86.6 1.4 gather_fusion.27
  88.0 1.4 gather_fusion.28
  89.4 1.4 fusion.61
  90.8 1.2 convolution_add_fusion.6
  92.0 1.2 convolution_add_fusion.5
  93.2 1.2 convolution_add_fusion.4
  94.3 1.1 convolution_bitcast_fusion.2
  95.4 1.1 convolution_bitcast_fusion.3
  97.7 1.4 gather_fusion.21
  99.1 1.7 fusion.53
  100.8 1.6 gather_fusion.22
  102.4 1.3 pad_clamp_fusion.5
  103.7 1.6 gather_fusion.23
  105.2 1.1 pad_maximum_fusion.2
  106.3 1.2 copy.100
  107.5 1.5 gather_fusion.24
  109.1 1.8 convolution_add_fusion.2
  110.9 1.5 convolution_add_fusion.1
  112.4 1.6 fusion.27
  115.9 1.8 copy.101
  118.9 0.9 gather_fusion.20
  119.8 2.9 %fusion.41 = f32[128,16,64]{2,0,1:T(8,128)} fusion(f32[128,16,64]{2,1,0:T(8,128)S(1)} %gather_fusion.20, f32[7,4,64,64]{3,2,1,0:T(8,128)} %param.14), kind=kOutput, calls=%fused_computation.102 | convolution fusion | flops 100663296 | bytes 1081344 | tf_op jit(solution)/shard_map/nvr,rs->nvs/dot_general | solution.py:52
  123.6 2.9 %fusion.43 = f32[128,16,64]{2,0,1:T(8,128)} fusion(f32[128,16,64]{2,1,0:T(8,128)S(1)} %gather_fusion.19, f32[7,4,64,64]{3,2,1,0:T(8,128)} %param.14), kind=kOutput, calls=%fused_computation.104 | convolution fusion | flops 100663296 | bytes 1081344 | tf_op jit(solution)/shard_map/nvr,rs->nvs/dot_general | solution.py:52
  128.1 2.9 %fusion.45 = f32[128,16,64]{2,0,1:T(8,128)} fusion(f32[128,16,64]{2,1,0:T(8,128)S(1)} %gather_fusion.18, f32[7,4,64,64]{3,2,1,0:T(8,128)} %param.14), kind=kOutput, calls=%fused_computation.106 | convolution fusion | flops 100663296 | bytes 1081344 | tf_op jit(solution)/shard_map/nvr,rs->nvs/dot_general | solution.py:52
  131.9 3.0 %fusion.47 = f32[128,16,64]{2,0,1:T(8,128)} fusion(f32[128,16,64]{2,1,0:T(8,128)S(1)} %gather_fusion.17, f32[7,4,64,64]{3,2,1,0:T(8,128)} %param.14), kind=kOutput, calls=%fused_computation.108 | convolution fusion | flops 100663296 | bytes 1081344 | tf_op jit(solution)/shard_map/nvr,rs->nvs/dot_general | solution.py:50
  134.9 1.1 dynamic-slice_add_fusion
  143.8 4.5 %collective-permute-start.3 = (f32[8,16,64]{2,1,0:T(8,128)}, f32[8,16,64]{2,1,0:T(8,128)S(1)}, u32[]{:S(2)}, u32[]{:S(2)}) collective-permute-start(f32[8,16,64]{2,1,0:T(8,128)} %convolution_add_fusion.11), channel_id=1, source_target_pairs={{4,0},{8,4},{12,8},{16,12},{20,16},{24,20},{28,24},{32,28},{36,32}... | collective-permute-start | bytes 98312 | tf_op jit(solution)/shard_map/ppermute | solution.py:21
  148.4 1.9 collective-permute-start
  151.6 0.9 fusion.82
  155.0 7.0 %collective-permute-start.1 = (f32[16,16,64]{2,1,0:T(8,128)S(1)}, f32[16,16,64]{2,1,0:T(8,128)}, u32[]{:S(2)}, u32[]{:S(2)}) collective-permute-start(f32[16,16,64]{2,1,0:T(8,128)S(1)} %copy-done.6), channel_id=1, source_target_pairs={{4,0},{8,4},{12,8},{16,12},{20,16},{24,20},{28,24},{32,28},{36,32}... | collective-permute-start | bytes 196616 | tf_op jit(solution)/shard_map/ppermute | solution.py:21
  162.0 1.9 collective-permute-start.8
  168.1 7.2 %collective-permute-start.9 = (f32[18,4096]{1,0:T(8,128)S(1)}, f32[18,4096]{1,0:T(8,128)}, u32[]{:S(2)}, u32[]{:S(2)}) collective-permute-start(f32[18,4096]{1,0:T(8,128)S(1)} %constant_dynamic-update-slice_fusion), channel_id=1, source_target_pairs={{4,0},{8,4},{12,8},{16,12},{20,16},{24,20},{28,24},{32,28},{36,32}... | collective-permute-start | bytes 884744 | tf_op jit(solution)/shard_map/ppermute | solution.py:21
  175.3 0.9 pad_maximum_fusion.4
  179.9 0.9 pad_maximum_fusion.3
  184.6 1.2 pad_maximum_fusion
  187.2 78.7 %while.10 = (s32[]{:T(128)}, f32[16,16,256]{2,1,0:T(8,128)S(1)}, s32[16]{0:T(128)S(1)}, s32[16,8]{1,0:T(8,128)}, f32[18,48,256]{2,0,1:T(8,128)S(1)}, /*index=5*/s32[]{:T(128)}, s32[1]{0:T(128)}) while((s32[]{:T(128)}, f32[16,16,256]{2,1,0:T(8,128)S(1)}, s32[16]{0:T(128)S(1)}, s32[16,8]{1,0:T(8,128)}, f32[18,48,256]{2,0,1:T(8,128)S(1)}, ...), condition=%wide.region_1.2_spmd, body=%wide.region_0.1_spmd.sunk | while | flops 117965864 | bytes 612669 | solution.py:105
  189.9 2.3 fusion.260
  194.8 2.3 fusion.260
  199.7 2.3 fusion.260
  204.6 2.3 fusion.260
  209.5 2.3 fusion.260
  214.5 2.3 fusion.260
  219.4 2.3 fusion.260
  224.3 2.3 fusion.260
  229.2 2.3 fusion.260
  234.1 2.3 fusion.260
  239.0 2.3 fusion.260
  244.0 2.3 fusion.260
  248.9 2.3 fusion.260
  253.8 2.3 fusion.260
  258.7 2.3 fusion.260
  263.6 2.3 fusion.260
  (276 shorter events, 73.1 us)
Async XLA Ops:
  0.0 1.2 copy-start
  0.0 3.1 %copy-start.4 = (f32[6,2,64,64]{3,2,1,0:T(8,128)S(1)}, f32[6,2,64,64]{3,2,1,0:T(8,128)}, u32[]{:S(2)}) copy-start(f32[6,2,64,64]{3,2,1,0:T(8,128)} %param.13) | copy-start | bytes 589828
  0.0 28.1 %copy-start.13 = (s32[3,128,4]{1,2,0:T(4,128)S(1)}, s32[3,128,4]{1,2,0:T(4,128)}, u32[]{:S(2)}) copy-start(s32[3,128,4]{1,2,0:T(4,128)} %param.17) | copy-start | bytes 18436
  3.1 75.8 %copy-start.5 = (f32[16,16,64]{2,1,0:T(8,128)}, f32[16,16,64]{2,1,0:T(8,128)S(1)}, u32[]{:S(2)}) copy-start(f32[16,16,64]{2,1,0:T(8,128)S(1)} %fusion.55) | copy-start | bytes 196612
  8.3 135.5 %collective-permute-start.6 = (f32[2,16,64]{2,1,0:T(8,128)S(1)}, f32[2,16,64]{2,1,0:T(8,128)}, u32[]{:S(2)}, u32[]{:S(2)}) collective-permute-start(f32[2,16,64]{2,1,0:T(8,128)S(1)} %convolution_add_fusion.15), channel_id=1, source_target_pairs={{0,4},{4,8},{8,12},{12,16},{16,20},{20,24},{24,28},{28,32},{32,36}... | collective-permute-start | bytes 24584 | tf_op jit(solution)/shard_map/ppermute | solution.py:19
  10.3 138.1 %collective-permute-start.7 = (f32[2,16,64]{2,1,0:T(8,128)S(1)}, f32[2,16,64]{2,1,0:T(8,128)}, u32[]{:S(2)}, u32[]{:S(2)}) collective-permute-start(f32[2,16,64]{2,1,0:T(8,128)S(1)} %convolution_add_fusion.15), channel_id=1, source_target_pairs={{4,0},{8,4},{12,8},{16,12},{20,16},{24,20},{28,24},{32,28},{36,32}... | collective-permute-start | bytes 24584 | tf_op jit(solution)/shard_map/ppermute | solution.py:21
  17.2 137.8 %collective-permute-start.4 = (f32[4,16,64]{2,1,0:T(8,128)}, f32[4,16,64]{2,1,0:T(8,128)}, u32[]{:S(2)}, u32[]{:S(2)}) collective-permute-start(f32[4,16,64]{2,1,0:T(8,128)} %convolution_add_fusion.13), channel_id=1, source_target_pairs={{0,4},{4,8},{8,12},{12,16},{16,20},{20,24},{24,28},{28,32},{32,36}... | collective-permute-start | bytes 49160 | tf_op jit(solution)/shard_map/ppermute | solution.py:19
  19.2 142.8 %collective-permute-start.5 = (f32[4,16,64]{2,1,0:T(8,128)}, f32[4,16,64]{2,1,0:T(8,128)}, u32[]{:S(2)}, u32[]{:S(2)}) collective-permute-start(f32[4,16,64]{2,1,0:T(8,128)} %convolution_add_fusion.13), channel_id=1, source_target_pairs={{4,0},{8,4},{12,8},{16,12},{20,16},{24,20},{28,24},{32,28},{36,32}... | collective-permute-start | bytes 49160 | tf_op jit(solution)/shard_map/ppermute | solution.py:21
  26.1 141.9 %collective-permute-start.2 = (f32[8,16,64]{2,1,0:T(8,128)}, f32[8,16,64]{2,1,0:T(8,128)}, u32[]{:S(2)}, u32[]{:S(2)}) collective-permute-start(f32[8,16,64]{2,1,0:T(8,128)} %convolution_add_fusion.11), channel_id=1, source_target_pairs={{0,4},{4,8},{8,12},{12,16},{16,20},{20,24},{24,28},{28,32},{32,36}... | collective-permute-start | bytes 98312 | tf_op jit(solution)/shard_map/ppermute | solution.py:19
  89.4 2.6 copy-start.7
  89.4 3.7 %copy-start.8 = (f32[32,16,64]{2,1,0:T(8,128)S(1)}, f32[32,16,64]{2,1,0:T(8,128)}, u32[]{:S(2)}) copy-start(f32[32,16,64]{2,1,0:T(8,128)} %gather_fusion.28) | copy-start | bytes 393220
  92.0 4.5 %copy-start.12 = (s32[64,4]{0,1:T(4,128)S(1)}, s32[64,4]{0,1:T(4,128)}, u32[]{:S(2)}) copy-start(s32[64,4]{0,1:T(4,128)} %slice_bitcast_fusion.17) | copy-start | bytes 3076
  109.1 1.8 copy-start.1
  110.8 1.5 copy-start.2
  110.9 1.5 copy-start.3
  123.6 3.0 %copy-start.14 = (s32[128]{0:T(128)S(1)}, s32[128]{0:T(128)}, u32[]{:S(2)}) copy-start(s32[128]{0:T(128)} %get-tuple-element.74) | copy-start | bytes 1540
  123.6 3.0 %copy-start.15 = (s32[128]{0:T(128)S(1)}, s32[128]{0:T(128)}, u32[]{:S(2)}) copy-start(s32[128]{0:T(128)} %get-tuple-element.77) | copy-start | bytes 1540
  131.9 4.5 %copy-start.9 = (f32[16,4096]{1,0:T(8,128)S(1)}, f32[16,4096]{1,0:T(8,128)}, u32[]{:S(2)}) copy-start(f32[16,4096]{1,0:T(8,128)} %param.10) | copy-start | bytes 786436
  131.9 16.4 %copy-start.6 = (f32[16,16,64]{2,1,0:T(8,128)S(1)}, f32[16,16,64]{2,1,0:T(8,128)}, u32[]{:S(2)}) copy-start(f32[16,16,64]{2,1,0:T(8,128)} %copy-done.5) | copy-start | bytes 196612
  134.9 18.1 %copy-start.10 = (f32[7,4,64,64]{3,2,1,0:T(8,128)S(1)}, f32[7,4,64,64]{3,2,1,0:T(8,128)}, u32[]{:S(2)}) copy-start(f32[7,4,64,64]{3,2,1,0:T(8,128)} %param.14) | copy-start | bytes 1376260
  143.8 31.5 %collective-permute-start.3 = (f32[8,16,64]{2,1,0:T(8,128)}, f32[8,16,64]{2,1,0:T(8,128)S(1)}, u32[]{:S(2)}, u32[]{:S(2)}) collective-permute-start(f32[8,16,64]{2,1,0:T(8,128)} %convolution_add_fusion.11), channel_id=1, source_target_pairs={{4,0},{8,4},{12,8},{16,12},{20,16},{24,20},{28,24},{32,28},{36,32}... | collective-permute-start | bytes 98312 | tf_op jit(solution)/shard_map/ppermute | solution.py:21
  148.4 31.5 %collective-permute-start = (f32[16,16,64]{2,1,0:T(8,128)S(1)}, f32[16,16,64]{2,1,0:T(8,128)S(1)}, u32[]{:S(2)}, u32[]{:S(2)}) collective-permute-start(f32[16,16,64]{2,1,0:T(8,128)S(1)} %copy-done.6), channel_id=1, source_target_pairs={{0,4},{4,8},{8,12},{12,16},{16,20},{20,24},{24,28},{28,32},{32,36}... | collective-permute-start | bytes 196616 | tf_op jit(solution)/shard_map/ppermute | solution.py:19
  155.0 24.8 %collective-permute-start.1 = (f32[16,16,64]{2,1,0:T(8,128)S(1)}, f32[16,16,64]{2,1,0:T(8,128)}, u32[]{:S(2)}, u32[]{:S(2)}) collective-permute-start(f32[16,16,64]{2,1,0:T(8,128)S(1)} %copy-done.6), channel_id=1, source_target_pairs={{4,0},{8,4},{12,8},{16,12},{20,16},{24,20},{28,24},{32,28},{36,32}... | collective-permute-start | bytes 196616 | tf_op jit(solution)/shard_map/ppermute | solution.py:21
  162.0 22.6 %collective-permute-start.8 = (f32[18,4096]{1,0:T(8,128)S(1)}, f32[18,4096]{1,0:T(8,128)}, u32[]{:S(2)}, u32[]{:S(2)}) collective-permute-start(f32[18,4096]{1,0:T(8,128)S(1)} %constant_dynamic-update-slice_fusion), channel_id=1, source_target_pairs={{0,4},{4,8},{8,12},{12,16},{16,20},{20,24},{24,28},{28,32},{32,36}... | collective-permute-start | bytes 884744 | tf_op jit(solution)/shard_map/ppermute | solution.py:19
  168.1 16.5 %collective-permute-start.9 = (f32[18,4096]{1,0:T(8,128)S(1)}, f32[18,4096]{1,0:T(8,128)}, u32[]{:S(2)}, u32[]{:S(2)}) collective-permute-start(f32[18,4096]{1,0:T(8,128)S(1)} %constant_dynamic-update-slice_fusion), channel_id=1, source_target_pairs={{4,0},{8,4},{12,8},{16,12},{20,16},{24,20},{28,24},{32,28},{36,32}... | collective-permute-start | bytes 884744 | tf_op jit(solution)/shard_map/ppermute | solution.py:21
  186.3 1.0 copy-start.11
where the time goes:
time: 270 us; the launch traced here: 267 us
  matrix products  78.1 us (29%)
  local copies, waits for them, and re-layouts  64.4 us (24%)
  blocking collectives  50 us (19%)
  starting transfers between devices  42.2 us (16%)
  other arithmetic  20.6 us (8%)
  loops' own time  11 us (4%)
    all_gather x1, blocking collectives, local(): every_cut = lax.all_gather(ups[levels_cut], 'leaf', axis=0, tiled=True)  50 us
    dot_general x16, matrix products, one_leaf(): return jnp.einsum('vjs,jst->vt', taken[:cols], weights, precision=highest)  36.4 us
    ppermute x5, starting transfers between devices, padded(): lax.ppermute(head, axis, [((i + 1) % count, i) for i in range(ends)])  32.6 us
    dot_general x21, matrix products, far_terms(): jnp.einsum('nvr,rs->nvs', source[rows[:, slot]], maps[slot], precision=hi...  20.1 us
    gather x21, local copies, waits for them, and re-layouts, far_terms(): source[rows[:, slot]]  17.9 us
    concatenate x16, local copies, waits for them, and re-layouts, one_leaf(): picks = jnp.concatenate([jnp.reshape(index + leaf_dev, (1,)), row])  11.1 us
    another operation x1, loops' own time, local(): near = lax.map(one_leaf, (jnp.arange(leaf_dev, dtype=jnp.int32), own_rows))  11 us
    ppermute x5, starting transfers between devices, padded(): lax.ppermute(tail, axis, [(i, (i + 1) % count) for i in range(ends)])  9.61 us
  transfers between devices with their start and end apart: 10, of which 0 were waited for; matrix products, arithmetic and copies ran while one was open for 31% of the time, Pallas kernels for 0%

commit v1 on v0

v1 whole, which is shorter than its diff:
```python
import jax
import jax.numpy as jnp
from jax import lax
from jax.experimental import pallas as pl
from jax.experimental.pallas import tpu as pltpu
from jax.sharding import PartitionSpec as P

MESH = pl.DeviceIdType.MESH
f32 = jnp.float32
bf16 = jnp.bfloat16
NT = (((1,), (1,)), ((), ()))

N_LEAF = 128
LEAVES = 16
LEAF = 256
RANK = 64
COLS = 16
NEAR = 8
FAR = 4
CUT = 4
SRC = NEAR + 1
SCALE = 5.0 * 1.4426950408889634
WEIGHT = 0.0625
TINY = 1e-30
BASE = (0, 16, 24, 28)
STRIP = 32


def split(x):
    high = x.astype(bf16)
    return high, (x - high.astype(f32)).astype(bf16)


def stacked(x):
    return jnp.concatenate(split(x), 0)


def fold(d):
    half = d.shape[0] // 2
    return d[:half] + d[half:]


def turned(x):
    return pltpu.roll(x, RANK, 1)


def low_lanes(shape):
    return lax.broadcasted_iota(jnp.int32, shape, 1) < RANK


def pick(a, b):
    return jnp.where(low_lanes(a.shape), a, b)


def both(r):
    return r + turned(r)


def halves(wide):
    high = wide.astype(bf16).astype(f32)
    return jnp.concatenate([high, wide - high], 1).astype(bf16)


def dot(a, b):
    return jnp.dot(a, b, preferred_element_type=f32)


def dot_t(a, b):
    return lax.dot_general(a, b, NT, preferred_element_type=f32)


def kernel(
    near_ref, far_ref, coarse_ref, vec_in, pts_in, bas_in, tra_in, cou_in,
    out_ref,
    vec, pts, bas, tra, cou, hv, hp, vh, rows, cols, buf_a, buf_b,
    ups, gath, tt, cc, bb, near_out,
    loc, hs, hr, us, ur, zs, zr, ys, yr, cs, cr,
):
    me = lax.axis_index("leaf")
    zi, yi, ci = me // 16, lax.rem(me // 2, 8), lax.rem(me, 2)
    left = lax.rem(me + N_LEAF - 1, N_LEAF)
    right = lax.rem(me + 1, N_LEAF)
    sibling = me + 1 - 2 * ci

    def z_peer(k):
        return lax.rem(zi + k, 8) * 16 + yi * 2 + ci

    def y_peer(k):
        return zi * 16 + lax.rem(yi + k, 8) * 2 + ci

    barrier = pltpu.get_barrier_semaphore()
    for peer in [left, right] + [z_peer(k) for k in range(1, 8)] + [y_peer(k) for k in range(1, 8)]:
        pl.semaphore_signal(barrier, inc=1, device_id={"leaf": peer}, device_id_type=MESH)

    locals_ = [
        pltpu.make_async_copy(src, dst, loc.at[i])
        for i, (src, dst) in enumerate(
            [(tra_in, tra), (cou_in, cou), (vec_in, vec), (bas_in, bas), (pts_in, pts)]
        )
    ]
    for copy in locals_:
        copy.start()

    def remote(src, dst, send, recv, peer):
        return pltpu.make_async_remote_copy(
            src_ref=src, dst_ref=dst, send_sem=send, recv_sem=recv,
            device_id={"leaf": peer}, device_id_type=MESH,
        )

    halo = [
        remote(vec_in, hv.at[0], hs.at[0], hr.at[0], right),
        remote(vec_in, hv.at[1], hs.at[1], hr.at[1], left),
        remote(pts_in, hp.at[0], hs.at[2], hr.at[2], right),
        remote(pts_in, hp.at[1], hs.at[3], hr.at[3], left),
    ]
    up_halo = [
        remote(ups.at[1], ups.at[0], us.at[0], ur.at[0], right),
        remote(ups.at[1], ups.at[2], us.at[1], ur.at[1], left),
    ]

    def z_copy(k):
        block = gath.at[zi, yi, ci]
        return remote(block, block, zs.at[k], zr.at[k], z_peer(k))

    def y_copy(k):
        block = gath.at[:, yi, ci]
        return remote(block, block, ys.at[k], yr.at[k], y_peer(k))

    half = gath.at[:, :, ci]
    c_copy = remote(half, half, cs, cr, sibling)

    locals_[0].wait()
    for k in range(6):
        for c in range(2):
            tt[k, c * RANK:(c + 1) * RANK, :] = halves(tra[k, c])

    pl.semaphore_wait(barrier, 16)
    for copy in halo:
        copy.start()

    locals_[2].wait()
    locals_[3].wait()
    level = []
    for leaf in range(LEAVES):
        s = stacked(vec[:, leaf * LEAF:(leaf + 1) * LEAF])
        vh[LEAVES + leaf] = jnp.concatenate([s, s], 1)
        b = stacked(bas[leaf])
        bb[leaf] = b
        level.append(both(fold(dot_t(s, b))))
    for k in range(CUT + 1):
        for n, u in enumerate(level):
            packed = pick(u[:8], u[8:])
            if k < CUT:
                ups[1, BASE[k] + n] = packed
            else:
                gath[zi, yi, ci] = packed
        if k < CUT:
            lhs = jnp.concatenate(
                [pick(level[2 * n], level[2 * n + 1]) for n in range(len(level) // 2)], 0
            )
            u = both(fold(dot(stacked(lhs), tt[k])))
            level = [u[n * COLS:(n + 1) * COLS] for n in range(len(level) // 2)]
    for k in range(1, 8):
        z_copy(k).start()
    for copy in up_halo:
        copy.start()

    locals_[1].wait()
    for k in range(7):
        for s in range(FAR):
            cc[k, s * RANK:(s + 1) * RANK, :] = halves(cou[k, s])

    def place(m, p):
        x = jnp.broadcast_to(p[0:1, :] * SCALE, (8, LEAF))
        y = jnp.broadcast_to(p[1:2, :] * SCALE, (8, LEAF))
        first = lax.broadcasted_iota(jnp.int32, (8, LEAF), 0) == 0
        cols[m, :, 0:8] = jnp.where(first, x, y).T
        return x, y

    locals_[4].wait()

    def own(i, _):
        at = pl.ds(pl.multiple_of(i * LEAF, LEAF), LEAF)
        x, y = place(LEAVES + i, pts[:, at])
        rows[i, 0] = x
        rows[i, 1] = y
        return 0

    lax.fori_loop(0, LEAVES, own, 0)
    for copy in halo:
        copy.wait_recv()

    def others(i, _):
        at = pl.ds(pl.multiple_of(i * LEAF, LEAF), LEAF)
        for side in range(2):
            m = 2 * LEAVES * side + i
            place(m, hp[side, :, at])
            s = stacked(hv[side, :, at])
            vh[m] = jnp.concatenate([s, s], 1)
        return 0

    lax.fori_loop(0, LEAVES, others, 0)

    first_leaf = (me - 1) * LEAVES

    def sources(t):
        return [LEAVES + t] + [
            jnp.clip(near_ref[j, t] - first_leaf, 0, 3 * LEAVES - 1) for j in range(NEAR)
        ]

    def weigh(t, buf):
        x = jnp.concatenate([rows[t, 0]] * (STRIP // 8), 0)
        y = jnp.concatenate([rows[t, 1]] * (STRIP // 8), 0)
        count = 0
        for j, m in enumerate(sources(t)):
            for r in range(0, LEAF, STRIP):
                sx = jnp.broadcast_to(cols[m, r:r + STRIP, 0:1], (STRIP, LEAF))
                sy = jnp.broadcast_to(cols[m, r:r + STRIP, 1:2], (STRIP, LEAF))
                dx, dy = sx - x, sy - y
                d2 = dx * dx + dy * dy
                if count % 4 < 3:
                    dist = pl.reciprocal(lax.rsqrt(d2), approx=True)
                else:
                    d2 = jnp.maximum(d2, TINY)
                    dist = d2 * lax.rsqrt(d2)
                count += 1
                high, low = split(jnp.exp2(-dist))
                at = j * 2 * LEAF + r
                buf[at:at + STRIP, :] = high
                buf[at + LEAF:at + LEAF + STRIP, :] = low

    def apply(t, buf):
        lhs = jnp.concatenate([vh[m] for m in sources(t)], 1)
        near_out[t] = fold(dot(lhs, buf[...])) * WEIGHT

    weigh(0, buf_a)

    def pair(i, _):
        @pl.when(i == 1)
        def _():
            for k in range(1, 8):
                z_copy(k).wait_recv()
            for k in range(1, 8):
                y_copy(k).start()

        @pl.when(i == 4)
        def _():
            for k in range(1, 8):
                y_copy(k).wait_recv()
            c_copy.start()

        apply(2 * i, buf_a)
        weigh(2 * i + 1, buf_b)
        apply(2 * i + 1, buf_b)
        weigh(2 * i + 2, buf_a)
        return 0

    lax.fori_loop(0, LEAVES // 2 - 1, pair, 0)

    for copy in up_halo:
        copy.wait_recv()
    c_copy.wait_recv()

    apply(LEAVES - 2, buf_a)
    weigh(LEAVES - 1, buf_b)
    apply(LEAVES - 1, buf_b)

    def four(xs):
        rs = [turned(x) for x in xs]
        return jnp.concatenate(
            [
                jnp.concatenate([pick(xs[s], rs[s + 1]), pick(rs[s], xs[s + 1])], 0)
                for s in (0, 2)
            ],
            1,
        )

    def cut_node(n):
        return gath[n // 16, lax.rem(n // 2, 8), lax.rem(n, 2)]

    def couple(lhs, k):
        return both(fold(dot(stacked(lhs), cc[k])))

    far = []
    for k in range(CUT):
        span = LEAVES >> k
        base = (me - 1) * span
        blocks = []
        for n in range(span):
            xs = []
            for s in range(FAR):
                at = jnp.clip(far_ref[k, s, n] - base, 0, 3 * span - 1)
                xs.append(ups[at // span, BASE[k] + lax.rem(at, span)])
            blocks.append(four(xs))
        far.append(couple(jnp.concatenate(blocks, 0), k))

    far_4 = couple(four([cut_node(coarse_ref[0, s, me]) for s in range(FAR)]), 4)

    def joined(n):
        a, b = cut_node(2 * n), cut_node(2 * n + 1)
        return jnp.concatenate([pick(a, turned(b)), pick(turned(a), b)], 0)

    mid, top = me // 2, me // 4
    blocks = [joined(coarse_ref[1, s, mid]) for s in range(FAR)]
    for s in range(FAR):
        n = coarse_ref[2, s, top]
        blocks += [joined(2 * n), joined(2 * n + 1)]
    u = both(fold(dot(stacked(jnp.concatenate(blocks, 0)), tt[4])))
    u = [u[n * COLS:(n + 1) * COLS] for n in range(12)]
    far_5 = couple(jnp.concatenate([pick(u[0], u[1]), pick(u[2], u[3])], 1), 5)
    lhs = jnp.concatenate([pick(u[4 + 2 * s], u[5 + 2 * s]) for s in range(FAR)], 0)
    u = both(fold(dot(stacked(lhs), tt[5])))
    u = [u[n * COLS:(n + 1) * COLS] for n in range(4)]
    down = couple(jnp.concatenate([pick(u[0], u[1]), pick(u[2], u[3])], 1), 6)

    def children(d, k):
        r = fold(dot_t(stacked(d), tt[k]))
        t = turned(r)
        return pick(r, t), pick(t, r)

    for k, node, here in ((5, mid, far_5), (4, me, far_4)):
        a, b = children(down, k)
        down = here + jnp.where(lax.rem(node, 2) == 0, a, b)
    for k in range(CUT - 1, -1, -1):
        a, b = children(down, k)
        parts = []
        for n in range(a.shape[0] // COLS):
            at = slice(n * COLS, (n + 1) * COLS)
            parts += [a[at], b[at]]
        down = far[k] + jnp.concatenate(parts, 0)

    for leaf in range(LEAVES):
        d = stacked(down[leaf * COLS:(leaf + 1) * COLS])
        out_ref[:, leaf * LEAF:(leaf + 1) * LEAF] = near_out[leaf] + fold(dot(d, bb[leaf]))

    for copy in halo + up_halo + [c_copy]:
        copy.wait_send()
    for k in range(1, 8):
        z_copy(k).wait_send()
        y_copy(k).wait_send()


def local(vectors, points, bases, transfer, coupling, near_lists, far_lists, coarse_lists):
    smem = pl.BlockSpec(memory_space=pltpu.SMEM)
    anywhere = pl.BlockSpec(memory_space=pl.ANY)
    vmem = pltpu.VMEM
    dma = pltpu.SemaphoreType.DMA
    return pl.pallas_call(
        kernel,
        out_shape=jax.ShapeDtypeStruct(vectors.shape, f32),
        in_specs=[smem] * 3 + [anywhere] * 5,
        out_specs=pl.BlockSpec(memory_space=vmem),
        scratch_shapes=[
            vmem((COLS, LEAVES * LEAF), f32),
            vmem((2, LEAVES * LEAF), f32),
            vmem((LEAVES, RANK, LEAF), f32),
            vmem((6, 2, RANK, RANK), f32),
            vmem((7, FAR, RANK, RANK), f32),
            vmem((2, COLS, LEAVES * LEAF), f32),
            vmem((2, 2, LEAVES * LEAF), f32),
            vmem((3 * LEAVES, 2 * COLS, 2 * LEAF), bf16),
            vmem((LEAVES, 2, 8, LEAF), f32),
            vmem((3 * LEAVES, LEAF, 128), f32),
            vmem((SRC * 2 * LEAF, LEAF), bf16),
            vmem((SRC * 2 * LEAF, LEAF), bf16),
            vmem((3, 30, 8, 128), f32),
            vmem((8, 8, 2, 8, 128), f32),
            vmem((6, 2 * RANK, 2 * RANK), bf16),
            vmem((7, FAR * RANK, 2 * RANK), bf16),
            vmem((LEAVES, 2 * RANK, LEAF), bf16),
            vmem((LEAVES, COLS, LEAF), f32),
            dma((5,)), dma((4,)), dma((4,)), dma((2,)), dma((2,)),
            dma((8,)), dma((8,)), dma((8,)), dma((8,)), dma, dma,
        ],
        compiler_params=pltpu.CompilerParams(
            collective_id=0, has_side_effects=True, vmem_limit_bytes=50 * 2**20
        ),
    )(
        near_lists.T,
        far_lists.transpose(0, 2, 1),
        coarse_lists.transpose(0, 2, 1),
        vectors,
        points,
        bases.transpose(0, 2, 1),
        transfer,
        coupling,
    )


def solution(mesh):
    in_specs = (
        P("vec", "leaf"),
        P(None, "leaf"),
        P("leaf", None, None),
        P(),
        P(),
        P("leaf", None),
        P(None, "leaf", None),
        P(),
    )
    return jax.shard_map(
        local, mesh=mesh, in_specs=in_specs, out_specs=P("vec", "leaf"), check_vma=False
    )
```

time: 270 us -> 53.9 us (0.20)
  the two profiles are of different devices: /device:TPU:260 before, /device:TPU:1 now
where the time goes in v1:
time: 53.9 us; the launch traced here: 53.5 us
  Pallas kernels  45.6 us (85%)
  local copies, waits for them, and re-layouts  7.88 us (15%)
    pallas_call x1, Pallas kernels, local(): pl.pallas_call(kernel, out_shape=jax.ShapeDtypeStruct(vectors.shape, f32)...  45.6 us
    unnamed x17, local copies, waits for them, and re-layouts  7.88 us

profile of v1, /device:TPU:1, one launch (start us, length us, event | category | flops | bytes accessed | tf_op | source)
XLA Modules:
  0.0 53.5 jit_solution(16019338321549367901)
XLA Ops:
  0.0 0.0 copy-start.6
  0.0 0.7 %copy-done.6 = s32[3,128,4]{1,2,0:T(4,128)S(1)} copy-done((s32[3,128,4]{1,2,0:T(4,128)S(1)}, s32[3,128,4]{1,2,0:T(4,128)}, u32[]{:S(2)}) %copy-start.6) | copy-done | bytes 6168
  0.7 0.0 copy-start
  0.7 1.2 %copy-done = f32[16,256,64]{1,2,0:T(8,128)S(1)} copy-done((f32[16,256,64]{1,2,0:T(8,128)S(1)}, f32[16,256,64]{1,2,0:T(8,128)}, u32[]{:S(2)}) %copy-start) | copy-done | bytes 1048600
  1.9 0.0 copy-start.1
  1.9 1.2 %copy-done.1 = f32[7,4,64,64]{3,2,1,0:T(8,128)S(1)} copy-done((f32[7,4,64,64]{3,2,1,0:T(8,128)S(1)}, f32[7,4,64,64]{3,2,1,0:T(8,128)}, u32[]{:S(2)}) %copy-start.1) | copy-done | bytes 458776
  3.1 0.0 copy-start.2
  3.1 1.0 %copy-done.2 = f32[6,2,64,64]{3,2,1,0:T(8,128)S(1)} copy-done((f32[6,2,64,64]{3,2,1,0:T(8,128)S(1)}, f32[6,2,64,64]{3,2,1,0:T(8,128)}, u32[]{:S(2)}) %copy-start.2) | copy-done | bytes 196632
  4.1 0.0 copy-start.3
  4.1 0.9 %copy-done.3 = f32[16,4096]{1,0:T(8,128)S(1)} copy-done((f32[16,4096]{1,0:T(8,128)S(1)}, f32[16,4096]{1,0:T(8,128)}, u32[]{:S(2)}) %copy-start.3) | copy-done | bytes 262168
  5.0 0.0 copy-start.4
  5.0 0.8 %copy-done.4 = f32[2,4096]{1,0:T(2,128)S(1)} copy-done((f32[2,4096]{1,0:T(2,128)S(1)}, f32[2,4096]{1,0:T(2,128)}, u32[]{:S(2)}) %copy-start.4) | copy-done | bytes 32792
  5.8 0.0 copy-start.5
  5.8 0.7 %copy-done.5 = s32[4,16,4]{1,2,0:T(4,128)S(1)} copy-done((s32[4,16,4]{1,2,0:T(4,128)S(1)}, s32[4,16,4]{1,2,0:T(4,128)}, u32[]{:S(2)}) %copy-start.5) | copy-done | bytes 1048
  6.5 0.0 copy-start.7
  6.5 0.7 %copy-done.7 = s32[16,8]{0,1:T(8,128)S(1)} copy-done((s32[16,8]{0,1:T(8,128)S(1)}, s32[16,8]{0,1:T(8,128)}, u32[]{:S(2)}) %copy-start.7) | copy-done | bytes 536
  7.2 45.6 %shard_map.82 = f32[16,4096]{1,0:T(8,128)S(1)} custom-call(s32[8,16]{1,0:T(8,128)S(1)} %bitcast.7, s32[4,4,16]{2,1,0:T(4,128)S(1)} %bitcast.5, s32[3,4,128]{2,1,0:T(4,128)S(1)} %bitcast.6, f32[16,4096]{1,0:T(8,128)S(1)} %copy-done.3, f32[2,4096]{1,0:T(2,128)S(1)} %copy-done.4, f32[16,64,256]{2,1,0:T(8,128)S(1)} %bitcast.4, f32[6,2,64,64]{3,2,1,0:T(8,128)S(1)} %copy-done.2, ...), custom_call_target="tpu_custom_call" | custom-call | tf_op jit(solution)/shard_map/pallas_call | solution.py:348
  52.8 0.7 %copy.10 = f32[16,4096]{1,0:T(8,128)} copy(f32[16,4096]{1,0:T(8,128)S(1)} %shard_map.82) | data formatting | bytes 524288
Async XLA Ops:
  0.0 0.7 %copy-start.6 = (s32[3,128,4]{1,2,0:T(4,128)S(1)}, s32[3,128,4]{1,2,0:T(4,128)}, u32[]{:S(2)}) copy-start(s32[3,128,4]{1,2,0:T(4,128)} %param.15) | copy-start | bytes 18436
  0.7 1.2 %copy-start = (f32[16,256,64]{1,2,0:T(8,128)S(1)}, f32[16,256,64]{1,2,0:T(8,128)}, u32[]{:S(2)}) copy-start(f32[16,256,64]{1,2,0:T(8,128)} %param.10) | copy-start | bytes 3145732
  1.9 1.2 %copy-start.1 = (f32[7,4,64,64]{3,2,1,0:T(8,128)S(1)}, f32[7,4,64,64]{3,2,1,0:T(8,128)}, u32[]{:S(2)}) copy-start(f32[7,4,64,64]{3,2,1,0:T(8,128)} %cou_in.1) | copy-start | bytes 1376260
  3.1 1.0 %copy-start.2 = (f32[6,2,64,64]{3,2,1,0:T(8,128)S(1)}, f32[6,2,64,64]{3,2,1,0:T(8,128)}, u32[]{:S(2)}) copy-start(f32[6,2,64,64]{3,2,1,0:T(8,128)} %tra_in.1) | copy-start | bytes 589828
  4.1 0.9 %copy-start.3 = (f32[16,4096]{1,0:T(8,128)S(1)}, f32[16,4096]{1,0:T(8,128)}, u32[]{:S(2)}) copy-start(f32[16,4096]{1,0:T(8,128)} %vec_in.1) | copy-start | bytes 786436
  5.0 0.8 %copy-start.4 = (f32[2,4096]{1,0:T(2,128)S(1)}, f32[2,4096]{1,0:T(2,128)}, u32[]{:S(2)}) copy-start(f32[2,4096]{1,0:T(2,128)} %pts_in.1) | copy-start | bytes 98308
  5.8 0.7 %copy-start.5 = (s32[4,16,4]{1,2,0:T(4,128)S(1)}, s32[4,16,4]{1,2,0:T(4,128)}, u32[]{:S(2)}) copy-start(s32[4,16,4]{1,2,0:T(4,128)} %param.14) | copy-start | bytes 3076
  6.5 0.7 %copy-start.7 = (s32[16,8]{0,1:T(8,128)S(1)}, s32[16,8]{0,1:T(8,128)}, u32[]{:S(2)}) copy-start(s32[16,8]{0,1:T(8,128)} %param.13) | copy-start | bytes 1540

commit v2 on v1

--- a/solution.py
+++ b/solution.py
@@ -1,3 +1,5 @@
+import functools
+
 import jax
 import jax.numpy as jnp
 from jax import lax
@@ -74,23 +76,32 @@
     out_ref,
     vec, pts, bas, tra, cou, hv, hp, vh, rows, cols, buf_a, buf_b,
     ups, gath, tt, cc, bb, near_out,
-    loc, hs, hr, us, ur, zs, zr, ys, yr, cs, cr,
+    loc, hs, hr, us, ur, zs, zr, ys, yr, cs, cr, chain,
 ):
     me = lax.axis_index("leaf")
     zi, yi, ci = me // 16, lax.rem(me // 2, 8), lax.rem(me, 2)
-    left = lax.rem(me + N_LEAF - 1, N_LEAF)
-    right = lax.rem(me + 1, N_LEAF)
+    left, right = me - 1, me + 1
     sibling = me + 1 - 2 * ci
-
-    def z_peer(k):
-        return lax.rem(zi + k, 8) * 16 + yi * 2 + ci
 
     def y_peer(k):
         return zi * 16 + lax.rem(yi + k, 8) * 2 + ci
 
+    def signal(sem, peer):
+        pl.semaphore_signal(sem, inc=1, device_id={"leaf": peer}, device_id_type=MESH)
+
+    beside = [
+        (me > 0, me - 1),
+        (me < N_LEAF - 1, me + 1),
+        (zi > 0, me - 16),
+        (zi < 7, me + 16),
+    ]
     barrier = pltpu.get_barrier_semaphore()
-    for peer in [left, right] + [z_peer(k) for k in range(1, 8)] + [y_peer(k) for k in range(1, 8)]:
-        pl.semaphore_signal(barrier, inc=1, device_id={"leaf": peer}, device_id_type=MESH)
+    for k in range(1, 8):
+        signal(barrier, y_peer(k))
+    greeted = 7
+    for there, peer in beside:
+        greeted += there.astype(jnp.int32)
+        pl.when(there)(functools.partial(signal, barrier, peer))
 
     locals_ = [
         pltpu.make_async_copy(src, dst, loc.at[i])
@@ -107,20 +118,44 @@
             device_id={"leaf": peer}, device_id_type=MESH,
         )
 
-    halo = [
+    to_right = [
         remote(vec_in, hv.at[0], hs.at[0], hr.at[0], right),
-        remote(vec_in, hv.at[1], hs.at[1], hr.at[1], left),
-        remote(pts_in, hp.at[0], hs.at[2], hr.at[2], right),
+        remote(pts_in, hp.at[0], hs.at[1], hr.at[1], right),
+    ]
+    to_left = [
+        remote(vec_in, hv.at[1], hs.at[2], hr.at[2], left),
         remote(pts_in, hp.at[1], hs.at[3], hr.at[3], left),
     ]
-    up_halo = [
-        remote(ups.at[1], ups.at[0], us.at[0], ur.at[0], right),
-        remote(ups.at[1], ups.at[2], us.at[1], ur.at[1], left),
-    ]
-
-    def z_copy(k):
+    up_right = [remote(ups.at[1], ups.at[0], us.at[0], ur.at[0], right)]
+    up_left = [remote(ups.at[1], ups.at[2], us.at[1], ur.at[1], left)]
+
+    def run(step, copies):
+        for copy in copies:
+            getattr(copy, step)()
+
+    def send(rightward, leftward, step):
+        pl.when(me < N_LEAF - 1)(functools.partial(run, step, rightward))
+        pl.when(me > 0)(functools.partial(run, step, leftward))
+
+    def receive(rightward, leftward):
+        pl.when(me > 0)(functools.partial(run, "wait_recv", rightward))
+        pl.when(me < N_LEAF - 1)(functools.partial(run, "wait_recv", leftward))
+
+    def z_send(to, step):
         block = gath.at[zi, yi, ci]
-        return remote(block, block, zs.at[k], zr.at[k], z_peer(k))
+        run(step, [remote(block, block, zs.at[to], zr.at[zi], to * 16 + yi * 2 + ci)])
+
+    def z_receive(source):
+        block = gath.at[source, yi, ci]
+        run("wait_recv", [remote(block, block, zs.at[source], zr.at[source], source * 16 + yi * 2 + ci)])
+
+    def lower(f, *args):
+        for z in range(7):
+            pl.when(z < zi)(functools.partial(f, z, *args))
+
+    def higher(f, *args):
+        for z in range(1, 8):
+            pl.when(z > zi)(functools.partial(f, z, *args))
 
     def y_copy(k):
         block = gath.at[:, yi, ci]
@@ -134,9 +169,14 @@
         for c in range(2):
             tt[k, c * RANK:(c + 1) * RANK, :] = halves(tra[k, c])
 
-    pl.semaphore_wait(barrier, 16)
-    for copy in halo:
-        copy.start()
+    pl.semaphore_wait(barrier, greeted)
+    send(to_right, to_left, "start")
+
+    @pl.when(zi > 0)
+    def _():
+        pl.semaphore_wait(chain, 1)
+
+    pl.when(zi < 7)(functools.partial(signal, chain, me + 16))
 
     locals_[2].wait()
     locals_[3].wait()
@@ -160,10 +200,8 @@
             )
             u = both(fold(dot(stacked(lhs), tt[k])))
             level = [u[n * COLS:(n + 1) * COLS] for n in range(len(level) // 2)]
-    for k in range(1, 8):
-        z_copy(k).start()
-    for copy in up_halo:
-        copy.start()
+    lower(z_send, "start")
+    send(up_right, up_left, "start")
 
     locals_[1].wait()
     for k in range(7):
@@ -187,8 +225,7 @@
         return 0
 
     lax.fori_loop(0, LEAVES, own, 0)
-    for copy in halo:
-        copy.wait_recv()
+    receive(to_right, to_left)
 
     def others(i, _):
         at = pl.ds(pl.multiple_of(i * LEAF, LEAF), LEAF)
@@ -236,14 +273,18 @@
     weigh(0, buf_a)
 
     def pair(i, _):
-        @pl.when(i == 1)
+        @pl.when(i == 3)
         def _():
-            for k in range(1, 8):
-                z_copy(k).wait_recv()
+            higher(z_receive)
+            higher(z_send, "start")
+
+        @pl.when(i == 4)
+        def _():
+            lower(z_receive)
             for k in range(1, 8):
                 y_copy(k).start()
 
-        @pl.when(i == 4)
+        @pl.when(i == 6)
         def _():
             for k in range(1, 8):
                 y_copy(k).wait_recv()
@@ -257,12 +298,11 @@
 
     lax.fori_loop(0, LEAVES // 2 - 1, pair, 0)
 
-    for copy in up_halo:
-        copy.wait_recv()
-    c_copy.wait_recv()
-
     apply(LEAVES - 2, buf_a)
     weigh(LEAVES - 1, buf_b)
+
+    receive(up_right, up_left)
+    c_copy.wait_recv()
     apply(LEAVES - 1, buf_b)
 
     def four(xs):
@@ -333,11 +373,13 @@
         d = stacked(down[leaf * COLS:(leaf + 1) * COLS])
         out_ref[:, leaf * LEAF:(leaf + 1) * LEAF] = near_out[leaf] + fold(dot(d, bb[leaf]))
 
-    for copy in halo + up_halo + [c_copy]:
-        copy.wait_send()
+    send(to_right, to_left, "wait_send")
+    send(up_right, up_left, "wait_send")
+    lower(z_send, "wait_send")
+    higher(z_send, "wait_send")
     for k in range(1, 8):
-        z_copy(k).wait_send()
         y_copy(k).wait_send()
+    c_copy.wait_send()
 
 
 def local(vectors, points, bases, transfer, coupling, near_lists, far_lists, coarse_lists):
@@ -371,9 +413,10 @@
             vmem((LEAVES, COLS, LEAF), f32),
             dma((5,)), dma((4,)), dma((4,)), dma((2,)), dma((2,)),
             dma((8,)), dma((8,)), dma((8,)), dma((8,)), dma, dma,
+            pltpu.SemaphoreType.REGULAR,
         ],
         compiler_params=pltpu.CompilerParams(
-            collective_id=0, has_side_effects=True, vmem_limit_bytes=50 * 2**20
+            collective_id=0, has_side_effects=True, vmem_limit_bytes=64 * 2**20 - 2**16
         ),
     )(
         near_lists.T,

time: 53.9 us -> 47.1 us (0.87)
  local copies, waits for them, and re-layouts: 7.88 us -> 1.67 us
    unnamed x17 -> x1, local copies, waits for them, and re-layouts: 7.88 us -> 1.67 us
where the time goes in v2:
time: 47.1 us; the launch traced here: 46.8 us
  Pallas kernels  45.1 us (96%)
  local copies, waits for them, and re-layouts  1.67 us (4%)
    pallas_call x1, Pallas kernels, local(): pl.pallas_call(kernel, out_shape=jax.ShapeDtypeStruct(vectors.shape, f32)...  45.1 us
    unnamed x1, local copies, waits for them, and re-layouts  1.67 us

profile of v2, /device:TPU:1, one launch (start us, length us, event | category | flops | bytes accessed | tf_op | source)
XLA Modules:
  0.0 46.8 jit_solution(11741753452357769367)
XLA Ops:
  0.0 45.1 %shard_map.82 = f32[16,4096]{1,0:T(8,128)} custom-call(s32[8,16]{1,0:T(8,128)} %bitcast.7, s32[4,4,16]{2,1,0:T(4,128)} %bitcast.5, s32[3,4,128]{2,1,0:T(4,128)} %bitcast.6, f32[16,4096]{1,0:T(8,128)} %vec_in.1, f32[2,4096]{1,0:T(2,128)} %pts_in.1, f32[16,64,256]{2,1,0:T(8,128)} %bitcast.4, f32[6,2,64,64]{3,2,1,0:T(8,128)} %tra_in.1, f32[7,4,64,64]{3,2,1,0:T(8,128)} %cou_in.1), custom_call_target="tpu_custom_call" | custom-call | tf_op jit(solution)/shard_map/pallas_call | solution.py:390
  45.2 1.7 %copy.10 = f32[16,4096]{1,0:T(8,128)} copy(f32[16,4096]{1,0:T(8,128)} %shard_map.82) | data formatting | bytes 524288

commit v3 on v2

--- a/solution.py
+++ b/solution.py
@@ -20,7 +20,6 @@
 NEAR = 8
 FAR = 4
 CUT = 4
-SRC = NEAR + 1
 SCALE = 5.0 * 1.4426950408889634
 WEIGHT = 0.0625
 TINY = 1e-30
@@ -72,8 +71,9 @@
 
 
 def kernel(
-    near_ref, far_ref, coarse_ref, vec_in, pts_in, bas_in, tra_in, cou_in,
+    near_in, far_in, coarse_in, vec_in, pts_in, bas_in, tra_in, cou_in,
     out_ref,
+    near_ref, far_ref, coarse_ref,
     vec, pts, bas, tra, cou, hv, hp, vh, rows, cols, buf_a, buf_b,
     ups, gath, tt, cc, bb, near_out,
     loc, hs, hr, us, ur, zs, zr, ys, yr, cs, cr, chain,
@@ -106,7 +106,10 @@
     locals_ = [
         pltpu.make_async_copy(src, dst, loc.at[i])
         for i, (src, dst) in enumerate(
-            [(tra_in, tra), (cou_in, cou), (vec_in, vec), (bas_in, bas), (pts_in, pts)]
+            [
+                (tra_in, tra), (cou_in, cou), (vec_in, vec), (bas_in, bas), (pts_in, pts),
+                (near_in, near_ref), (far_in, far_ref), (coarse_in, coarse_ref),
+            ]
         )
     ]
     for copy in locals_:
@@ -142,11 +145,11 @@
         pl.when(me < N_LEAF - 1)(functools.partial(run, "wait_recv", leftward))
 
     def z_send(to, step):
-        block = gath.at[zi, yi, ci]
+        block = gath.at[zi, ci]
         run(step, [remote(block, block, zs.at[to], zr.at[zi], to * 16 + yi * 2 + ci)])
 
     def z_receive(source):
-        block = gath.at[source, yi, ci]
+        block = gath.at[source, ci]
         run("wait_recv", [remote(block, block, zs.at[source], zr.at[source], source * 16 + yi * 2 + ci)])
 
     def lower(f, *args):
@@ -158,11 +161,20 @@
             pl.when(z > zi)(functools.partial(f, z, *args))
 
     def y_copy(k):
-        block = gath.at[:, yi, ci]
+        block = gath.at[zi, ci, yi]
         return remote(block, block, ys.at[k], yr.at[k], y_peer(k))
 
-    half = gath.at[:, :, ci]
-    c_copy = remote(half, half, cs, cr, sibling)
+    def y_receive(k):
+        block = gath.at[zi, ci, lax.rem(yi + 8 - k, 8)]
+        run("wait_recv", [remote(block, block, ys.at[k], yr.at[k], y_peer(8 - k))])
+
+    def c_send(z, step):
+        block = gath.at[z, ci]
+        run(step, [remote(block, block, cs.at[z], cr.at[z], sibling)])
+
+    def c_receive(z):
+        block = gath.at[z, 1 - ci]
+        run("wait_recv", [remote(block, block, cs.at[z], cr.at[z], sibling)])
 
     locals_[0].wait()
     for k in range(6):
@@ -193,14 +205,15 @@
             if k < CUT:
                 ups[1, BASE[k] + n] = packed
             else:
-                gath[zi, yi, ci] = packed
+                gath[zi, ci, yi] = packed
         if k < CUT:
             lhs = jnp.concatenate(
                 [pick(level[2 * n], level[2 * n + 1]) for n in range(len(level) // 2)], 0
             )
             u = both(fold(dot(stacked(lhs), tt[k])))
             level = [u[n * COLS:(n + 1) * COLS] for n in range(len(level) // 2)]
-    lower(z_send, "start")
+    for k in range(1, 8):
+        y_copy(k).start()
     send(up_right, up_left, "start")
 
     locals_[1].wait()
@@ -215,60 +228,79 @@
         cols[m, :, 0:8] = jnp.where(first, x, y).T
         return x, y
 
+    def weights(x, y, m, put):
+        x = jnp.concatenate([x] * (STRIP // 8), 0)
+        y = jnp.concatenate([y] * (STRIP // 8), 0)
+        for r in range(0, LEAF, STRIP):
+            sx = jnp.broadcast_to(cols[m, r:r + STRIP, 0:1], (STRIP, LEAF))
+            sy = jnp.broadcast_to(cols[m, r:r + STRIP, 1:2], (STRIP, LEAF))
+            dx, dy = sx - x, sy - y
+            d2 = dx * dx + dy * dy
+            if (r // STRIP) % 4 < 3:
+                dist = pl.reciprocal(lax.rsqrt(d2), approx=True)
+            else:
+                d2 = jnp.maximum(d2, TINY)
+                dist = d2 * lax.rsqrt(d2)
+            put(r, *split(jnp.exp2(-dist)))
+
     locals_[4].wait()
 
     def own(i, _):
-        at = pl.ds(pl.multiple_of(i * LEAF, LEAF), LEAF)
-        x, y = place(LEAVES + i, pts[:, at])
-        rows[i, 0] = x
-        rows[i, 1] = y
+        for n in range(4):
+            t = i * 4 + n
+            x, y = place(LEAVES + t, pts[:, pl.ds(pl.multiple_of(t * LEAF, LEAF), LEAF)])
+            rows[t, 0] = x
+            rows[t, 1] = y
+            highs, lows = [], []
+
+            def put(r, high, low):
+                highs.append(high)
+                lows.append(low)
+
+            weights(x, y, LEAVES + t, put)
+            near_out[t] = fold(dot(vh[LEAVES + t], jnp.concatenate(highs + lows, 0)))
         return 0
 
-    lax.fori_loop(0, LEAVES, own, 0)
+    lax.fori_loop(0, LEAVES // 4, own, 0)
+    for k in range(1, 8):
+        y_receive(k)
+    lower(z_send, "start")
+    c_send(zi, "start")
+    for copy in locals_[5:]:
+        copy.wait()
     receive(to_right, to_left)
 
     def others(i, _):
-        at = pl.ds(pl.multiple_of(i * LEAF, LEAF), LEAF)
-        for side in range(2):
-            m = 2 * LEAVES * side + i
-            place(m, hp[side, :, at])
-            s = stacked(hv[side, :, at])
-            vh[m] = jnp.concatenate([s, s], 1)
+        for n in range(4):
+            t = i * 4 + n
+            at = pl.ds(pl.multiple_of(t * LEAF, LEAF), LEAF)
+            for side in range(2):
+                m = 2 * LEAVES * side + t
+                place(m, hp[side, :, at])
+                s = stacked(hv[side, :, at])
+                vh[m] = jnp.concatenate([s, s], 1)
         return 0
 
-    lax.fori_loop(0, LEAVES, others, 0)
+    lax.fori_loop(0, LEAVES // 4, others, 0)
 
     first_leaf = (me - 1) * LEAVES
 
     def sources(t):
-        return [LEAVES + t] + [
+        return [
             jnp.clip(near_ref[j, t] - first_leaf, 0, 3 * LEAVES - 1) for j in range(NEAR)
         ]
 
     def weigh(t, buf):
-        x = jnp.concatenate([rows[t, 0]] * (STRIP // 8), 0)
-        y = jnp.concatenate([rows[t, 1]] * (STRIP // 8), 0)
-        count = 0
         for j, m in enumerate(sources(t)):
-            for r in range(0, LEAF, STRIP):
-                sx = jnp.broadcast_to(cols[m, r:r + STRIP, 0:1], (STRIP, LEAF))
-                sy = jnp.broadcast_to(cols[m, r:r + STRIP, 1:2], (STRIP, LEAF))
-                dx, dy = sx - x, sy - y
-                d2 = dx * dx + dy * dy
-                if count % 4 < 3:
-                    dist = pl.reciprocal(lax.rsqrt(d2), approx=True)
-                else:
-                    d2 = jnp.maximum(d2, TINY)
-                    dist = d2 * lax.rsqrt(d2)
-                count += 1
-                high, low = split(jnp.exp2(-dist))
-                at = j * 2 * LEAF + r
-                buf[at:at + STRIP, :] = high
-                buf[at + LEAF:at + LEAF + STRIP, :] = low
+            def put(r, high, low, at=j * 2 * LEAF):
+                buf[at + r:at + r + STRIP, :] = high
+                buf[at + LEAF + r:at + LEAF + r + STRIP, :] = low
+
+            weights(rows[t, 0], rows[t, 1], m, put)
 
     def apply(t, buf):
         lhs = jnp.concatenate([vh[m] for m in sources(t)], 1)
-        near_out[t] = fold(dot(lhs, buf[...])) * WEIGHT
+        near_out[t] = (near_out[t] + fold(dot(lhs, buf[...]))) * WEIGHT
 
     weigh(0, buf_a)
 
@@ -277,18 +309,12 @@
         def _():
             higher(z_receive)
             higher(z_send, "start")
-
-        @pl.when(i == 4)
+            higher(c_send, "start")
+
+        @pl.when(i == 5)
         def _():
             lower(z_receive)
-            for k in range(1, 8):
-                y_copy(k).start()
-
-        @pl.when(i == 6)
-        def _():
-            for k in range(1, 8):
-                y_copy(k).wait_recv()
-            c_copy.start()
+            lower(c_send, "start")
 
         apply(2 * i, buf_a)
         weigh(2 * i + 1, buf_b)
@@ -298,12 +324,11 @@
 
     lax.fori_loop(0, LEAVES // 2 - 1, pair, 0)
 
+    receive(up_right, up_left)
+    for z in range(8):
+        c_receive(z)
     apply(LEAVES - 2, buf_a)
     weigh(LEAVES - 1, buf_b)
-
-    receive(up_right, up_left)
-    c_copy.wait_recv()
-    apply(LEAVES - 1, buf_b)
 
     def four(xs):
         rs = [turned(x) for x in xs]
@@ -316,7 +341,7 @@
         )
 
     def cut_node(n):
-        return gath[n // 16, lax.rem(n // 2, 8), lax.rem(n, 2)]
+        return gath[n // 16, lax.rem(n, 2), lax.rem(n // 2, 8)]
 
     def couple(lhs, k):
         return both(fold(dot(stacked(lhs), cc[k])))
@@ -369,6 +394,7 @@
             parts += [a[at], b[at]]
         down = far[k] + jnp.concatenate(parts, 0)
 
+    apply(LEAVES - 1, buf_b)
     for leaf in range(LEAVES):
         d = stacked(down[leaf * COLS:(leaf + 1) * COLS])
         out_ref[:, leaf * LEAF:(leaf + 1) * LEAF] = near_out[leaf] + fold(dot(d, bb[leaf]))
@@ -379,20 +405,24 @@
     higher(z_send, "wait_send")
     for k in range(1, 8):
         y_copy(k).wait_send()
-    c_copy.wait_send()
+    for z in range(8):
+        c_send(z, "wait_send")
 
 
 def local(vectors, points, bases, transfer, coupling, near_lists, far_lists, coarse_lists):
-    smem = pl.BlockSpec(memory_space=pltpu.SMEM)
-    anywhere = pl.BlockSpec(memory_space=pl.ANY)
+    outside = pl.BlockSpec(memory_space=pltpu.HBM)
+    smem = pltpu.SMEM
     vmem = pltpu.VMEM
     dma = pltpu.SemaphoreType.DMA
     return pl.pallas_call(
         kernel,
         out_shape=jax.ShapeDtypeStruct(vectors.shape, f32),
-        in_specs=[smem] * 3 + [anywhere] * 5,
+        in_specs=[outside] * 8,
         out_specs=pl.BlockSpec(memory_space=vmem),
         scratch_shapes=[
+            smem((NEAR, LEAVES), jnp.int32),
+            smem((CUT, FAR, LEAVES), jnp.int32),
+            smem((3, FAR, N_LEAF), jnp.int32),
             vmem((COLS, LEAVES * LEAF), f32),
             vmem((2, LEAVES * LEAF), f32),
             vmem((LEAVES, RANK, LEAF), f32),
@@ -403,20 +433,20 @@
             vmem((3 * LEAVES, 2 * COLS, 2 * LEAF), bf16),
             vmem((LEAVES, 2, 8, LEAF), f32),
             vmem((3 * LEAVES, LEAF, 128), f32),
-            vmem((SRC * 2 * LEAF, LEAF), bf16),
-            vmem((SRC * 2 * LEAF, LEAF), bf16),
+            vmem((NEAR * 2 * LEAF, LEAF), bf16),
+            vmem((NEAR * 2 * LEAF, LEAF), bf16),
             vmem((3, 30, 8, 128), f32),
-            vmem((8, 8, 2, 8, 128), f32),
+            vmem((8, 2, 8, 8, 128), f32),
             vmem((6, 2 * RANK, 2 * RANK), bf16),
             vmem((7, FAR * RANK, 2 * RANK), bf16),
             vmem((LEAVES, 2 * RANK, LEAF), bf16),
             vmem((LEAVES, COLS, LEAF), f32),
-            dma((5,)), dma((4,)), dma((4,)), dma((2,)), dma((2,)),
-            dma((8,)), dma((8,)), dma((8,)), dma((8,)), dma, dma,
+            dma((8,)), dma((4,)), dma((4,)), dma((2,)), dma((2,)),
+            dma((8,)), dma((8,)), dma((8,)), dma((8,)), dma((8,)), dma((8,)),
             pltpu.SemaphoreType.REGULAR,
         ],
         compiler_params=pltpu.CompilerParams(
-            collective_id=0, has_side_effects=True, vmem_limit_bytes=64 * 2**20 - 2**16
+            collective_id=0, has_side_effects=True, vmem_limit_bytes=48 * 2**20
         ),
     )(
         near_lists.T,

time: 47.1 us -> 46.7 us (level)
  the two profiles are of different devices: /device:TPU:1 before, /device:TPU:6 now
where the time goes in v3:
time: 46.7 us; the launch traced here: 46.3 us
  Pallas kernels  38.4 us (82%)
  local copies, waits for them, and re-layouts  7.88 us (17%)
    pallas_call x1, Pallas kernels, local(): pl.pallas_call(kernel, out_shape=jax.ShapeDtypeStruct(vectors.shape, f32)...  38.4 us
    unnamed x17, local copies, waits for them, and re-layouts  7.88 us

profile of v3, /device:TPU:6, one launch (start us, length us, event | category | flops | bytes accessed | tf_op | source)
XLA Modules:
  0.0 46.3 jit_solution(15651871918894841159)
XLA Ops:
  0.0 0.0 copy-start.6
  0.0 0.7 %copy-done.6 = s32[3,128,4]{1,2,0:T(4,128)S(1)} copy-done((s32[3,128,4]{1,2,0:T(4,128)S(1)}, s32[3,128,4]{1,2,0:T(4,128)}, u32[]{:S(2)}) %copy-start.6) | copy-done | bytes 6168
  0.7 0.0 copy-start
  0.7 1.2 %copy-done = f32[16,256,64]{1,2,0:T(8,128)S(1)} copy-done((f32[16,256,64]{1,2,0:T(8,128)S(1)}, f32[16,256,64]{1,2,0:T(8,128)}, u32[]{:S(2)}) %copy-start) | copy-done | bytes 1048600
  1.9 0.0 copy-start.1
  1.9 1.2 %copy-done.1 = f32[7,4,64,64]{3,2,1,0:T(8,128)S(1)} copy-done((f32[7,4,64,64]{3,2,1,0:T(8,128)S(1)}, f32[7,4,64,64]{3,2,1,0:T(8,128)}, u32[]{:S(2)}) %copy-start.1) | copy-done | bytes 458776
  3.1 0.0 copy-start.2
  3.1 1.0 %copy-done.2 = f32[6,2,64,64]{3,2,1,0:T(8,128)S(1)} copy-done((f32[6,2,64,64]{3,2,1,0:T(8,128)S(1)}, f32[6,2,64,64]{3,2,1,0:T(8,128)}, u32[]{:S(2)}) %copy-start.2) | copy-done | bytes 196632
  4.1 0.0 copy-start.3
  4.1 0.9 %copy-done.3 = f32[16,4096]{1,0:T(8,128)S(1)} copy-done((f32[16,4096]{1,0:T(8,128)S(1)}, f32[16,4096]{1,0:T(8,128)}, u32[]{:S(2)}) %copy-start.3) | copy-done | bytes 262168
  5.0 0.0 copy-start.4
  5.0 0.8 %copy-done.4 = f32[2,4096]{1,0:T(2,128)S(1)} copy-done((f32[2,4096]{1,0:T(2,128)S(1)}, f32[2,4096]{1,0:T(2,128)}, u32[]{:S(2)}) %copy-start.4) | copy-done | bytes 32792
  5.8 0.0 copy-start.5
  5.8 0.7 %copy-done.5 = s32[4,16,4]{1,2,0:T(4,128)S(1)} copy-done((s32[4,16,4]{1,2,0:T(4,128)S(1)}, s32[4,16,4]{1,2,0:T(4,128)}, u32[]{:S(2)}) %copy-start.5) | copy-done | bytes 1048
  6.5 0.0 copy-start.7
  6.5 0.7 %copy-done.7 = s32[16,8]{0,1:T(8,128)S(1)} copy-done((s32[16,8]{0,1:T(8,128)S(1)}, s32[16,8]{0,1:T(8,128)}, u32[]{:S(2)}) %copy-start.7) | copy-done | bytes 536
  7.2 38.4 %shard_map.82 = f32[16,4096]{1,0:T(8,128)S(1)} custom-call(s32[8,16]{1,0:T(8,128)S(1)} %bitcast.7, s32[4,4,16]{2,1,0:T(4,128)S(1)} %bitcast.5, s32[3,4,128]{2,1,0:T(4,128)S(1)} %bitcast.6, f32[16,4096]{1,0:T(8,128)S(1)} %copy-done.3, f32[2,4096]{1,0:T(2,128)S(1)} %copy-done.4, f32[16,64,256]{2,1,0:T(8,128)S(1)} %bitcast.4, f32[6,2,64,64]{3,2,1,0:T(8,128)S(1)} %copy-done.2, ...), custom_call_target="tpu_custom_call" | custom-call | tf_op jit(solution)/shard_map/pallas_call | solution.py:417
  45.6 0.7 %copy.10 = f32[16,4096]{1,0:T(8,128)} copy(f32[16,4096]{1,0:T(8,128)S(1)} %shard_map.82) | data formatting | bytes 524288
Async XLA Ops:
  0.0 0.7 %copy-start.6 = (s32[3,128,4]{1,2,0:T(4,128)S(1)}, s32[3,128,4]{1,2,0:T(4,128)}, u32[]{:S(2)}) copy-start(s32[3,128,4]{1,2,0:T(4,128)} %param.15) | copy-start | bytes 18436
  0.7 1.2 %copy-start = (f32[16,256,64]{1,2,0:T(8,128)S(1)}, f32[16,256,64]{1,2,0:T(8,128)}, u32[]{:S(2)}) copy-start(f32[16,256,64]{1,2,0:T(8,128)} %param.10) | copy-start | bytes 3145732
  1.9 1.2 %copy-start.1 = (f32[7,4,64,64]{3,2,1,0:T(8,128)S(1)}, f32[7,4,64,64]{3,2,1,0:T(8,128)}, u32[]{:S(2)}) copy-start(f32[7,4,64,64]{3,2,1,0:T(8,128)} %cou_in.1) | copy-start | bytes 1376260
  3.1 1.0 %copy-start.2 = (f32[6,2,64,64]{3,2,1,0:T(8,128)S(1)}, f32[6,2,64,64]{3,2,1,0:T(8,128)}, u32[]{:S(2)}) copy-start(f32[6,2,64,64]{3,2,1,0:T(8,128)} %tra_in.1) | copy-start | bytes 589828
  4.1 0.9 %copy-start.3 = (f32[16,4096]{1,0:T(8,128)S(1)}, f32[16,4096]{1,0:T(8,128)}, u32[]{:S(2)}) copy-start(f32[16,4096]{1,0:T(8,128)} %vec_in.1) | copy-start | bytes 786436
  5.0 0.8 %copy-start.4 = (f32[2,4096]{1,0:T(2,128)S(1)}, f32[2,4096]{1,0:T(2,128)}, u32[]{:S(2)}) copy-start(f32[2,4096]{1,0:T(2,128)} %pts_in.1) | copy-start | bytes 98308
  5.8 0.7 %copy-start.5 = (s32[4,16,4]{1,2,0:T(4,128)S(1)}, s32[4,16,4]{1,2,0:T(4,128)}, u32[]{:S(2)}) copy-start(s32[4,16,4]{1,2,0:T(4,128)} %param.14) | copy-start | bytes 3076
  6.5 0.7 %copy-start.7 = (s32[16,8]{0,1:T(8,128)S(1)}, s32[16,8]{0,1:T(8,128)}, u32[]{:S(2)}) copy-start(s32[16,8]{0,1:T(8,128)} %param.13) | copy-start | bytes 1540

commit v4 on v3

--- a/solution.py
+++ b/solution.py
@@ -24,6 +24,7 @@
 WEIGHT = 0.0625
 TINY = 1e-30
 BASE = (0, 16, 24, 28)
+NODES = 30
 STRIP = 32
 
 
@@ -76,7 +77,7 @@
     near_ref, far_ref, coarse_ref,
     vec, pts, bas, tra, cou, hv, hp, vh, rows, cols, buf_a, buf_b,
     ups, gath, tt, cc, bb, near_out,
-    loc, hs, hr, us, ur, zs, zr, ys, yr, cs, cr, chain,
+    loc, hs, hr, us, ur, zs, zr, ys, yr, cs, cr, chain, here,
 ):
     me = lax.axis_index("leaf")
     zi, yi, ci = me // 16, lax.rem(me // 2, 8), lax.rem(me, 2)
@@ -129,8 +130,9 @@
         remote(vec_in, hv.at[1], hs.at[2], hr.at[2], left),
         remote(pts_in, hp.at[1], hs.at[3], hr.at[3], left),
     ]
-    up_right = [remote(ups.at[1], ups.at[0], us.at[0], ur.at[0], right)]
-    up_left = [remote(ups.at[1], ups.at[2], us.at[1], ur.at[1], left)]
+    mine = ups.at[NODES:2 * NODES]
+    up_right = [remote(mine, ups.at[0:NODES], us.at[0], ur.at[0], right)]
+    up_left = [remote(mine, ups.at[2 * NODES:3 * NODES], us.at[1], ur.at[1], left)]
 
     def run(step, copies):
         for copy in copies:
@@ -144,14 +146,6 @@
         pl.when(me > 0)(functools.partial(run, "wait_recv", rightward))
         pl.when(me < N_LEAF - 1)(functools.partial(run, "wait_recv", leftward))
 
-    def z_send(to, step):
-        block = gath.at[zi, ci]
-        run(step, [remote(block, block, zs.at[to], zr.at[zi], to * 16 + yi * 2 + ci)])
-
-    def z_receive(source):
-        block = gath.at[source, ci]
-        run("wait_recv", [remote(block, block, zs.at[source], zr.at[source], source * 16 + yi * 2 + ci)])
-
     def lower(f, *args):
         for z in range(7):
             pl.when(z < zi)(functools.partial(f, z, *args))
@@ -160,35 +154,54 @@
         for z in range(1, 8):
             pl.when(z > zi)(functools.partial(f, z, *args))
 
-    def y_copy(k):
-        block = gath.at[zi, ci, yi]
-        return remote(block, block, ys.at[k], yr.at[k], y_peer(k))
-
-    def y_receive(k):
-        block = gath.at[zi, ci, lax.rem(yi + 8 - k, 8)]
-        run("wait_recv", [remote(block, block, ys.at[k], yr.at[k], y_peer(8 - k))])
-
-    def c_send(z, step):
-        block = gath.at[z, ci]
-        run(step, [remote(block, block, cs.at[z], cr.at[z], sibling)])
-
-    def c_receive(z):
-        block = gath.at[z, 1 - ci]
-        run("wait_recv", [remote(block, block, cs.at[z], cr.at[z], sibling)])
+    def z_block(core, z):
+        return gath.at[z, 0] if core == 0 else gath.at[z, 1, yi]
+
+    def y_block(core, y):
+        return gath.at[zi, 0, y] if core == 0 else gath.at[:, 1, y]
+
+    def z_send(to, core, step):
+        block = z_block(core, zi)
+        run(step, [remote(block, block, zs.at[to], zr.at[zi], to * 16 + yi * 2 + core)])
+
+    def z_receive(source, core):
+        block = z_block(core, source)
+        peer = source * 16 + yi * 2 + core
+        run("wait_recv", [remote(block, block, zs.at[source], zr.at[source], peer)])
+
+    def y_send(core, step):
+        block = y_block(core, yi)
+        for k in range(1, 8):
+            run(step, [remote(block, block, ys.at[k], yr.at[k], y_peer(k))])
+
+    def y_receive(core):
+        for k in range(1, 8):
+            block = y_block(core, lax.rem(yi + 8 - k, 8))
+            run("wait_recv", [remote(block, block, ys.at[k], yr.at[k], y_peer(8 - k))])
+
+    def on_core(core, *steps):
+        def go():
+            for f, *args in steps:
+                f(*args)
+
+        pl.when(ci == core)(go)
+
+    half, other = gath.at[:, ci], gath.at[:, 1 - ci]
+    c_send = remote(half, half, cs, cr, sibling)
+    c_receive = remote(other, other, cs, cr, sibling)
+
+    first = (me == 0) & (lax.axis_index("vec") == 0)
+
+    def enter():
+        pl.semaphore_wait(barrier, greeted)
+        send(to_right, to_left, "start")
+
+    pl.when(first)(enter)
 
     locals_[0].wait()
     for k in range(6):
         for c in range(2):
             tt[k, c * RANK:(c + 1) * RANK, :] = halves(tra[k, c])
-
-    pl.semaphore_wait(barrier, greeted)
-    send(to_right, to_left, "start")
-
-    @pl.when(zi > 0)
-    def _():
-        pl.semaphore_wait(chain, 1)
-
-    pl.when(zi < 7)(functools.partial(signal, chain, me + 16))
 
     locals_[2].wait()
     locals_[3].wait()
@@ -203,7 +216,7 @@
         for n, u in enumerate(level):
             packed = pick(u[:8], u[8:])
             if k < CUT:
-                ups[1, BASE[k] + n] = packed
+                ups[NODES + BASE[k] + n] = packed
             else:
                 gath[zi, ci, yi] = packed
         if k < CUT:
@@ -212,9 +225,18 @@
             )
             u = both(fold(dot(stacked(lhs), tt[k])))
             level = [u[n * COLS:(n + 1) * COLS] for n in range(len(level) // 2)]
-    for k in range(1, 8):
-        y_copy(k).start()
+    pl.when(jnp.logical_not(first))(enter)
+    on_core(0, (y_send, 0, "start"))
     send(up_right, up_left, "start")
+
+    @pl.when(zi > 0)
+    def _():
+        pl.semaphore_wait(chain, 1)
+
+    pl.when(zi < 7)(functools.partial(signal, chain, me + 16))
+    for z in range(7):
+        pl.when(z < zi)(functools.partial(signal, here, z * 16 + yi * 2 + ci))
+    on_core(1, (lower, z_send, 1, "start"))
 
     locals_[1].wait()
     for k in range(7):
@@ -246,8 +268,8 @@
     locals_[4].wait()
 
     def own(i, _):
-        for n in range(4):
-            t = i * 4 + n
+        for n in range(8):
+            t = i * 8 + n
             x, y = place(LEAVES + t, pts[:, pl.ds(pl.multiple_of(t * LEAF, LEAF), LEAF)])
             rows[t, 0] = x
             rows[t, 1] = y
@@ -261,11 +283,7 @@
             near_out[t] = fold(dot(vh[LEAVES + t], jnp.concatenate(highs + lows, 0)))
         return 0
 
-    lax.fori_loop(0, LEAVES // 4, own, 0)
-    for k in range(1, 8):
-        y_receive(k)
-    lower(z_send, "start")
-    c_send(zi, "start")
+    lax.fori_loop(0, LEAVES // 8, own, 0)
     for copy in locals_[5:]:
         copy.wait()
     receive(to_right, to_left)
@@ -305,16 +323,25 @@
     weigh(0, buf_a)
 
     def pair(i, _):
-        @pl.when(i == 3)
+        @pl.when(i == 0)
         def _():
-            higher(z_receive)
-            higher(z_send, "start")
-            higher(c_send, "start")
-
-        @pl.when(i == 5)
+            on_core(0, (y_receive, 0), (lower, z_send, 0, "start"))
+
+        @pl.when((i == 2) & (zi < 7))
         def _():
-            lower(z_receive)
-            lower(c_send, "start")
+            pl.semaphore_wait(here, 7 - zi)
+            on_core(0, (higher, z_send, 0, "start"))
+            on_core(1, (higher, z_send, 1, "start"))
+
+        @pl.when(i == 2)
+        def _():
+            on_core(1, (higher, z_receive, 1), (lower, z_receive, 1), (y_send, 1, "start"))
+
+        @pl.when(i == 6 - 2 * first.astype(jnp.int32))
+        def _():
+            on_core(0, (higher, z_receive, 0), (lower, z_receive, 0))
+            on_core(1, (y_receive, 1))
+            c_send.start()
 
         apply(2 * i, buf_a)
         weigh(2 * i + 1, buf_b)
@@ -325,8 +352,7 @@
     lax.fori_loop(0, LEAVES // 2 - 1, pair, 0)
 
     receive(up_right, up_left)
-    for z in range(8):
-        c_receive(z)
+    c_receive.wait_recv()
     apply(LEAVES - 2, buf_a)
     weigh(LEAVES - 1, buf_b)
 
@@ -341,7 +367,7 @@
         )
 
     def cut_node(n):
-        return gath[n // 16, lax.rem(n, 2), lax.rem(n // 2, 8)]
+        return gath[n >> 4, n & 1, (n >> 1) & 7]
 
     def couple(lhs, k):
         return both(fold(dot(stacked(lhs), cc[k])))
@@ -355,7 +381,8 @@
             xs = []
             for s in range(FAR):
                 at = jnp.clip(far_ref[k, s, n] - base, 0, 3 * span - 1)
-                xs.append(ups[at // span, BASE[k] + lax.rem(at, span)])
+                side = at >> (CUT - k)
+                xs.append(ups[at + side * (NODES - span) + BASE[k]])
             blocks.append(four(xs))
         far.append(couple(jnp.concatenate(blocks, 0), k))
 
@@ -401,12 +428,14 @@
 
     send(to_right, to_left, "wait_send")
     send(up_right, up_left, "wait_send")
-    lower(z_send, "wait_send")
-    higher(z_send, "wait_send")
-    for k in range(1, 8):
-        y_copy(k).wait_send()
-    for z in range(8):
-        c_send(z, "wait_send")
+    for core in range(2):
+        on_core(
+            core,
+            (lower, z_send, core, "wait_send"),
+            (higher, z_send, core, "wait_send"),
+            (y_send, core, "wait_send"),
+        )
+    c_send.wait_send()
 
 
 def local(vectors, points, bases, transfer, coupling, near_lists, far_lists, coarse_lists):
@@ -435,18 +464,18 @@
             vmem((3 * LEAVES, LEAF, 128), f32),
             vmem((NEAR * 2 * LEAF, LEAF), bf16),
             vmem((NEAR * 2 * LEAF, LEAF), bf16),
-            vmem((3, 30, 8, 128), f32),
+            vmem((3 * NODES, 8, 128), f32),
             vmem((8, 2, 8, 8, 128), f32),
             vmem((6, 2 * RANK, 2 * RANK), bf16),
             vmem((7, FAR * RANK, 2 * RANK), bf16),
             vmem((LEAVES, 2 * RANK, LEAF), bf16),
             vmem((LEAVES, COLS, LEAF), f32),
             dma((8,)), dma((4,)), dma((4,)), dma((2,)), dma((2,)),
-            dma((8,)), dma((8,)), dma((8,)), dma((8,)), dma((8,)), dma((8,)),
-            pltpu.SemaphoreType.REGULAR,
+            dma((8,)), dma((8,)), dma((8,)), dma((8,)), dma, dma,
+            pltpu.SemaphoreType.REGULAR, pltpu.SemaphoreType.REGULAR,
         ],
         compiler_params=pltpu.CompilerParams(
-            collective_id=0, has_side_effects=True, vmem_limit_bytes=48 * 2**20
+            collective_id=0, has_side_effects=True, vmem_limit_bytes=62 * 2**20
         ),
     )(
         near_lists.T,

time: 46.7 us -> 37.6 us (0.81)
  the two profiles are of different devices: /device:TPU:6 before, /device:TPU:1 now
where the time goes in v4:
time: 37.6 us; the launch traced here: 36.9 us
  Pallas kernels  35.2 us (94%)
  local copies, waits for them, and re-layouts  1.67 us (4%)
    pallas_call x1, Pallas kernels, local(): pl.pallas_call(kernel, out_shape=jax.ShapeDtypeStruct(vectors.shape, f32)...  35.2 us
    unnamed x1, local copies, waits for them, and re-layouts  1.67 us

profile of v4, /device:TPU:1, one launch (start us, length us, event | category | flops | bytes accessed | tf_op | source)
XLA Modules:
  0.0 36.9 jit_solution(6270676513375654770)
XLA Ops:
  0.0 35.2 %shard_map.82 = f32[16,4096]{1,0:T(8,128)} custom-call(s32[8,16]{1,0:T(8,128)} %bitcast.7, s32[4,4,16]{2,1,0:T(4,128)} %bitcast.5, s32[3,4,128]{2,1,0:T(4,128)} %bitcast.6, f32[16,4096]{1,0:T(8,128)} %vec_in.1, f32[2,4096]{1,0:T(2,128)} %pts_in.1, f32[16,64,256]{2,1,0:T(8,128)} %bitcast.4, f32[6,2,64,64]{3,2,1,0:T(8,128)} %tra_in.1, f32[7,4,64,64]{3,2,1,0:T(8,128)} %cou_in.1), custom_call_target="tpu_custom_call" | custom-call | tf_op jit(solution)/shard_map/pallas_call | solution.py:446
  35.2 1.7 %copy.10 = f32[16,4096]{1,0:T(8,128)} copy(f32[16,4096]{1,0:T(8,128)} %shard_map.82) | data formatting | bytes 524288

commit v5 on v4

--- a/solution.py
+++ b/solution.py
@@ -123,12 +123,12 @@
         )
 
     to_right = [
+        remote(pts_in, hp.at[0], hs.at[1], hr.at[1], right),
         remote(vec_in, hv.at[0], hs.at[0], hr.at[0], right),
-        remote(pts_in, hp.at[0], hs.at[1], hr.at[1], right),
     ]
     to_left = [
+        remote(pts_in, hp.at[1], hs.at[3], hr.at[3], left),
         remote(vec_in, hv.at[1], hs.at[2], hr.at[2], left),
-        remote(pts_in, hp.at[1], hs.at[3], hr.at[3], left),
     ]
     mine = ups.at[NODES:2 * NODES]
     up_right = [remote(mine, ups.at[0:NODES], us.at[0], ur.at[0], right)]
@@ -138,9 +138,22 @@
         for copy in copies:
             getattr(copy, step)()
 
+    def on_core(core, *steps):
+        def go():
+            for f, *args in steps:
+                f(*args)
+
+        pl.when(ci == core)(go)
+
     def send(rightward, leftward, step):
-        pl.when(me < N_LEAF - 1)(functools.partial(run, step, rightward))
-        pl.when(me > 0)(functools.partial(run, step, leftward))
+        def go_right():
+            pl.when(me < N_LEAF - 1)(functools.partial(run, step, rightward))
+
+        def go_left():
+            pl.when(me > 0)(functools.partial(run, step, leftward))
+
+        on_core(0, (go_left,), (go_right,))
+        on_core(1, (go_right,), (go_left,))
 
     def receive(rightward, leftward):
         pl.when(me > 0)(functools.partial(run, "wait_recv", rightward))
@@ -178,13 +191,6 @@
         for k in range(1, 8):
             block = y_block(core, lax.rem(yi + 8 - k, 8))
             run("wait_recv", [remote(block, block, ys.at[k], yr.at[k], y_peer(8 - k))])
-
-    def on_core(core, *steps):
-        def go():
-            for f, *args in steps:
-                f(*args)
-
-        pl.when(ci == core)(go)
 
     half, other = gath.at[:, ci], gath.at[:, 1 - ci]
     c_send = remote(half, half, cs, cr, sibling)
@@ -286,7 +292,7 @@
     lax.fori_loop(0, LEAVES // 8, own, 0)
     for copy in locals_[5:]:
         copy.wait()
-    receive(to_right, to_left)
+    receive(to_right[:1], to_left[:1])
 
     def others(i, _):
         for n in range(4):
@@ -295,8 +301,6 @@
             for side in range(2):
                 m = 2 * LEAVES * side + t
                 place(m, hp[side, :, at])
-                s = stacked(hv[side, :, at])
-                vh[m] = jnp.concatenate([s, s], 1)
         return 0
 
     lax.fori_loop(0, LEAVES // 4, others, 0)
@@ -321,6 +325,18 @@
         near_out[t] = (near_out[t] + fold(dot(lhs, buf[...]))) * WEIGHT
 
     weigh(0, buf_a)
+    receive(to_right[1:], to_left[1:])
+
+    def parts(i, _):
+        for n in range(8):
+            t = i * 8 + n
+            at = pl.ds(pl.multiple_of(t * LEAF, LEAF), LEAF)
+            for side in range(2):
+                s = stacked(hv[side, :, at])
+                vh[2 * LEAVES * side + t] = jnp.concatenate([s, s], 1)
+        return 0
+
+    lax.fori_loop(0, LEAVES // 8, parts, 0)
 
     def pair(i, _):
         @pl.when(i == 0)
@@ -333,7 +349,7 @@
             on_core(0, (higher, z_send, 0, "start"))
             on_core(1, (higher, z_send, 1, "start"))
 
-        @pl.when(i == 2)
+        @pl.when(i == 3)
         def _():
             on_core(1, (higher, z_receive, 1), (lower, z_receive, 1), (y_send, 1, "start"))
 

time: 37.6 us -> 36.5 us (0.971)
  the two profiles are of different devices: /device:TPU:1 before, /device:TPU:8 now
where the time goes in v5:
time: 36.5 us; the launch traced here: 36.3 us
  Pallas kernels  34.6 us (95%)
  local copies, waits for them, and re-layouts  1.67 us (5%)
    pallas_call x1, Pallas kernels, local(): pl.pallas_call(kernel, out_shape=jax.ShapeDtypeStruct(vectors.shape, f32)...  34.6 us
    unnamed x1, local copies, waits for them, and re-layouts  1.67 us

profile of v5, /device:TPU:8, one launch (start us, length us, event | category | flops | bytes accessed | tf_op | source)
XLA Modules:
  0.0 36.3 jit_solution(15627432204760327692)
XLA Ops:
  0.0 34.6 %shard_map.82 = f32[16,4096]{1,0:T(8,128)} custom-call(s32[8,16]{1,0:T(8,128)} %bitcast.7, s32[4,4,16]{2,1,0:T(4,128)} %bitcast.5, s32[3,4,128]{2,1,0:T(4,128)} %bitcast.6, f32[16,4096]{1,0:T(8,128)} %vec_in.1, f32[2,4096]{1,0:T(2,128)} %pts_in.1, f32[16,64,256]{2,1,0:T(8,128)} %bitcast.4, f32[6,2,64,64]{3,2,1,0:T(8,128)} %tra_in.1, f32[7,4,64,64]{3,2,1,0:T(8,128)} %cou_in.1), custom_call_target="tpu_custom_call" | custom-call | tf_op jit(solution)/shard_map/pallas_call | solution.py:462
  34.6 1.7 %copy.10 = f32[16,4096]{1,0:T(8,128)} copy(f32[16,4096]{1,0:T(8,128)} %shard_map.82) | data formatting | bytes 524288

commit v6 on v5

--- a/solution.py
+++ b/solution.py
@@ -77,7 +77,7 @@
     near_ref, far_ref, coarse_ref,
     vec, pts, bas, tra, cou, hv, hp, vh, rows, cols, buf_a, buf_b,
     ups, gath, tt, cc, bb, near_out,
-    loc, hs, hr, us, ur, zs, zr, ys, yr, cs, cr, chain, here,
+    loc, hs, hr, us, ur, zs, zr, ys, yr, cs, cr, chain, here, late,
 ):
     me = lax.axis_index("leaf")
     zi, yi, ci = me // 16, lax.rem(me // 2, 8), lax.rem(me, 2)
@@ -96,10 +96,18 @@
         (zi > 0, me - 16),
         (zi < 7, me + 16),
     ]
+    vi = lax.axis_index("vec")
+    first = (me == 0) & (vi == 0)
+    after_first = (zi == 0) & (ci == 0) & (yi > 0) & (vi == 0)
+
     barrier = pltpu.get_barrier_semaphore()
-    for k in range(1, 8):
-        signal(barrier, y_peer(k))
-    greeted = 7
+
+    def greet_y(sem):
+        for k in range(1, 8):
+            signal(sem, y_peer(k))
+
+    pl.when(jnp.logical_not(first))(functools.partial(greet_y, barrier))
+    greeted = 7 - after_first.astype(jnp.int32)
     for there, peer in beside:
         greeted += there.astype(jnp.int32)
         pl.when(there)(functools.partial(signal, barrier, peer))
@@ -187,6 +195,21 @@
         for k in range(1, 8):
             run(step, [remote(block, block, ys.at[k], yr.at[k], y_peer(k))])
 
+    def y_to(k):
+        block = y_block(0, yi)
+        remote(block, block, ys.at[k], yr.at[k], y_peer(k)).start()
+
+    def y_early():
+        for k in range(1, 8):
+            put_off = after_first & (lax.rem(yi + k, 8) == 0)
+            pl.when(jnp.logical_not(put_off))(functools.partial(y_to, k))
+
+    def y_late():
+        @pl.when(after_first)
+        def _():
+            pl.semaphore_wait(late, 1)
+            y_to(8 - yi)
+
     def y_receive(core):
         for k in range(1, 8):
             block = y_block(core, lax.rem(yi + 8 - k, 8))
@@ -196,11 +219,10 @@
     c_send = remote(half, half, cs, cr, sibling)
     c_receive = remote(other, other, cs, cr, sibling)
 
-    first = (me == 0) & (lax.axis_index("vec") == 0)
-
     def enter():
         pl.semaphore_wait(barrier, greeted)
         send(to_right, to_left, "start")
+        pl.when(first)(functools.partial(greet_y, late))
 
     pl.when(first)(enter)
 
@@ -231,18 +253,23 @@
             )
             u = both(fold(dot(stacked(lhs), tt[k])))
             level = [u[n * COLS:(n + 1) * COLS] for n in range(len(level) // 2)]
-    pl.when(jnp.logical_not(first))(enter)
-    on_core(0, (y_send, 0, "start"))
-    send(up_right, up_left, "start")
-
-    @pl.when(zi > 0)
-    def _():
-        pl.semaphore_wait(chain, 1)
-
-    pl.when(zi < 7)(functools.partial(signal, chain, me + 16))
-    for z in range(7):
-        pl.when(z < zi)(functools.partial(signal, here, z * 16 + yi * 2 + ci))
-    on_core(1, (lower, z_send, 1, "start"))
+    patient = (yi == 0) & jnp.logical_not(first)
+
+    def greet():
+        pl.when(jnp.logical_not(first))(enter)
+        on_core(0, (y_early,))
+        send(up_right, up_left, "start")
+
+        @pl.when(zi > 0)
+        def _():
+            pl.semaphore_wait(chain, 1)
+
+        pl.when(zi < 7)(functools.partial(signal, chain, me + 16))
+        for z in range(7):
+            pl.when(z < zi)(functools.partial(signal, here, z * 16 + yi * 2 + ci))
+        on_core(1, (lower, z_send, 1, "start"))
+
+    pl.when(jnp.logical_not(patient))(greet)
 
     locals_[1].wait()
     for k in range(7):
@@ -289,7 +316,11 @@
             near_out[t] = fold(dot(vh[LEAVES + t], jnp.concatenate(highs + lows, 0)))
         return 0
 
-    lax.fori_loop(0, LEAVES // 8, own, 0)
+    def own_part(i, _):
+        pl.when((i == 1) & patient)(greet)
+        return own(i, _)
+
+    lax.fori_loop(0, LEAVES // 8, own_part, 0)
     for copy in locals_[5:]:
         copy.wait()
     receive(to_right[:1], to_left[:1])
@@ -341,7 +372,7 @@
     def pair(i, _):
         @pl.when(i == 0)
         def _():
-            on_core(0, (y_receive, 0), (lower, z_send, 0, "start"))
+            on_core(0, (y_late,), (y_receive, 0), (lower, z_send, 0, "start"))
 
         @pl.when((i == 2) & (zi < 7))
         def _():
@@ -489,6 +520,7 @@
             dma((8,)), dma((4,)), dma((4,)), dma((2,)), dma((2,)),
             dma((8,)), dma((8,)), dma((8,)), dma((8,)), dma, dma,
             pltpu.SemaphoreType.REGULAR, pltpu.SemaphoreType.REGULAR,
+            pltpu.SemaphoreType.REGULAR,
         ],
         compiler_params=pltpu.CompilerParams(
             collective_id=0, has_side_effects=True, vmem_limit_bytes=62 * 2**20

time: 36.5 us -> 34.9 us (0.956)
  the two profiles are of different devices: /device:TPU:8 before, /device:TPU:255 now
where the time goes in v6:
time: 34.9 us; the launch traced here: 34.8 us
  Pallas kernels  33.1 us (95%)
  local copies, waits for them, and re-layouts  1.67 us (5%)
    pallas_call x1, Pallas kernels, local(): pl.pallas_call(kernel, out_shape=jax.ShapeDtypeStruct(vectors.shape, f32)...  33.1 us
    unnamed x1, local copies, waits for them, and re-layouts  1.67 us

profile of v6, /device:TPU:255, one launch (start us, length us, event | category | flops | bytes accessed | tf_op | source)
XLA Modules:
  0.0 34.8 jit_solution(2285792899962765040)
XLA Ops:
  0.0 33.1 %shard_map.82 = f32[16,4096]{1,0:T(8,128)} custom-call(s32[8,16]{1,0:T(8,128)} %bitcast.7, s32[4,4,16]{2,1,0:T(4,128)} %bitcast.5, s32[3,4,128]{2,1,0:T(4,128)} %bitcast.6, f32[16,4096]{1,0:T(8,128)} %vec_in.1, f32[2,4096]{1,0:T(2,128)} %pts_in.1, f32[16,64,256]{2,1,0:T(8,128)} %bitcast.4, f32[6,2,64,64]{3,2,1,0:T(8,128)} %tra_in.1, f32[7,4,64,64]{3,2,1,0:T(8,128)} %cou_in.1), custom_call_target="tpu_custom_call" | custom-call | tf_op jit(solution)/shard_map/pallas_call | solution.py:493
  33.1 1.7 %copy.10 = f32[16,4096]{1,0:T(8,128)} copy(f32[16,4096]{1,0:T(8,128)} %shard_map.82) | data formatting | bytes 524288

commit v7 on v6

--- a/solution.py
+++ b/solution.py
@@ -253,7 +253,7 @@
             )
             u = both(fold(dot(stacked(lhs), tt[k])))
             level = [u[n * COLS:(n + 1) * COLS] for n in range(len(level) // 2)]
-    patient = (yi == 0) & jnp.logical_not(first)
+    patient = (yi < 2) & jnp.logical_not(first)
 
     def greet():
         pl.when(jnp.logical_not(first))(enter)
@@ -471,7 +471,7 @@
     apply(LEAVES - 1, buf_b)
     for leaf in range(LEAVES):
         d = stacked(down[leaf * COLS:(leaf + 1) * COLS])
-        out_ref[:, leaf * LEAF:(leaf + 1) * LEAF] = near_out[leaf] + fold(dot(d, bb[leaf]))
+        out_ref[leaf] = near_out[leaf] + fold(dot(d, bb[leaf]))
 
     send(to_right, to_left, "wait_send")
     send(up_right, up_left, "wait_send")
@@ -490,9 +490,9 @@
     smem = pltpu.SMEM
     vmem = pltpu.VMEM
     dma = pltpu.SemaphoreType.DMA
-    return pl.pallas_call(
+    by_leaf = pl.pallas_call(
         kernel,
-        out_shape=jax.ShapeDtypeStruct(vectors.shape, f32),
+        out_shape=jax.ShapeDtypeStruct((LEAVES, COLS, LEAF), f32),
         in_specs=[outside] * 8,
         out_specs=pl.BlockSpec(memory_space=vmem),
         scratch_shapes=[
@@ -535,6 +535,7 @@
         transfer,
         coupling,
     )
+    return by_leaf.transpose(1, 0, 2).reshape(vectors.shape)
 
 
 def solution(mesh):

time: 34.9 us -> 34.9 us (level)
    unnamed x1 -> x0, local copies, waits for them, and re-layouts: 1.67 us -> none
    reshape x0 -> x1, local copies, waits for them, and re-layouts: none -> 1.67 us  [local(): return by_leaf.transpose(1, 0, 2).reshape(vectors.shape)]
where the time goes in v7:
time: 34.9 us; the launch traced here: 34.8 us
  Pallas kernels  33.1 us (95%)
  local copies, waits for them, and re-layouts  1.67 us (5%)
    pallas_call x1, Pallas kernels, local(): pl.pallas_call(kernel, out_shape=jax.ShapeDtypeStruct((LEAVES, COLS, LEAF...  33.1 us
    reshape x1, local copies, waits for them, and re-layouts, local(): return by_leaf.transpose(1, 0, 2).reshape(vectors.shape)  1.67 us

profile of v7, /device:TPU:255, one launch (start us, length us, event | category | flops | bytes accessed | tf_op | source)
XLA Modules:
  0.0 34.8 jit_solution(4047872897528525970)
XLA Ops:
  0.0 33.1 %shard_map.82 = f32[16,16,256]{2,1,0:T(8,128)} custom-call(s32[8,16]{1,0:T(8,128)} %bitcast.11, s32[4,4,16]{2,1,0:T(4,128)} %bitcast.9, s32[3,4,128]{2,1,0:T(4,128)} %bitcast.10, f32[16,4096]{1,0:T(8,128)} %vec_in.1, f32[2,4096]{1,0:T(2,128)} %pts_in.1, f32[16,64,256]{2,1,0:T(8,128)} %bitcast.8, f32[6,2,64,64]{3,2,1,0:T(8,128)} %tra_in.1, ...), custom_call_target="tpu_custom_call" | custom-call | tf_op jit(solution)/shard_map/pallas_call | solution.py:493
  33.1 1.7 %copy.10 = f32[16,2,8,256]{3,2,0,1:T(8,128)} copy(f32[16,2,8,256]{3,2,1,0:T(8,128)} %bitcast.7) | data formatting | bytes 524288 | tf_op jit(solution)/shard_map/reshape | solution.py:538
